TPU v7x, 128 devices: a whole 4x4x4 slice. The times are simulated.
128 devices in a mesh: arch: 4 (over y), clus: 32 (over x, z, core).
Axes of the slice: x: 4, y: 4, z: 4, core: 2. Of those that a mesh axis runs over, the one named last changes fastest.
Arguments:
- windows: bfloat16 [4096, 16, 3, 400], P(('arch', 'clus')), may hold values from -40 to 40
- pick_mask: int32 [4096, 16], P(('arch', 'clus')), may hold values 0 or 1
- band_member: int32 [16], replicated, may hold values 0 or 1
- event_owner: int32 [4096], replicated, may hold values from 0 to 31, as said below
- partners: int32 [4096, 32], replicated, may hold values from 0 to 4095, as said below
Outputs:
- correlation: bfloat16 [8192, 32, 16, 128], P('clus', None, 'arch')
Inputs may be any that keep to these rules, and one draw needn't show every extreme that they name: `event_owner`: within each aligned block of 32 events (one archive shard), at most 2 events name the same owner, and some owner is named by exactly 2 events in every block. `partners`: every partner's owner is the event's own owner or the next one, (owner + 1) mod 32.
All inputs are finite; a program needn't handle non-finite values. No bound on the sum of `pick_mask` on one device may be relied on, other than what follows from the above.
Results may differ from a plain program's by a relative error of at most 0.0052.
Values may be sent and summed in bfloat16 or wider, within the bound.
A program may use at most 64 MiB of HBM per device.

v0:
```python
import math

import jax
import jax.numpy as jnp
from jax import lax
from jax.sharding import PartitionSpec as P

L = 400
COMP = 3
K = 128
K0 = 16
LAGS = 128


EPSILON = 1e-06


def from_behind(block, axis, distance):
    devices = range(lax.axis_size(axis))
    route = [((i - distance) % len(devices), i) for i in devices]
    return lax.ppermute(block, axis, route)


def forward_table():
    samples = jnp.arange(L, dtype=jnp.int32)
    bins = jnp.arange(K, dtype=jnp.int32) + K0
    turns = samples[:, None] * bins[None, :] % (2 * L)
    phase = turns.astype(jnp.float32) * (math.pi / L)
    taper = 0.5 - 0.5 * jnp.cos((samples.astype(jnp.float32) + 0.5) * (2.0 * math.pi / L))
    table = jnp.concatenate(
        [taper[:, None] * jnp.cos(phase), -taper[:, None] * jnp.sin(phase)], axis=1
    )
    return table.astype(jnp.bfloat16)


def inverse_table():
    bins = jnp.arange(K, dtype=jnp.int32) + K0
    shifts = jnp.arange(LAGS, dtype=jnp.int32) - LAGS // 2
    turns = jnp.remainder(bins[:, None] * shifts[None, :], 2 * L)
    phase = turns.astype(jnp.float32) * (math.pi / L)
    return jnp.concatenate([jnp.cos(phase), -jnp.sin(phase)], axis=0).astype(jnp.bfloat16)


def transform(samples, table):
    flat = samples.reshape(-1, samples.shape[-1])
    spec = jnp.dot(flat, table, preferred_element_type=jnp.float32).astype(jnp.bfloat16)
    return spec.reshape(samples.shape[:-1] + (table.shape[1],))


def slot_layout(event_owner, device_count, block_events, owner_slots, capacity):
    blocks = event_owner.reshape(device_count, block_events)
    same_owner = blocks[:, :, None] == blocks[:, None, :]
    positions = jnp.arange(block_events, dtype=jnp.int32)
    earlier = positions[None, :] < positions[:, None]
    ranks = jnp.sum((same_owner & earlier[None]).astype(jnp.int32), axis=2)
    sources = jnp.arange(device_count, dtype=jnp.int32)[:, None]
    return (blocks * owner_slots + sources * capacity + ranks).reshape(-1)


def correlate(near, far, near_energy, far_energy, band_scale, inverse):
    near_real = near[..., :K].astype(jnp.float32)
    near_imag = near[..., K:].astype(jnp.float32)
    far_real = far[..., :K].astype(jnp.float32)
    far_imag = far[..., K:].astype(jnp.float32)
    real_part = jnp.sum(near_real * far_real + near_imag * far_imag, axis=2)
    imag_part = jnp.sum(near_imag * far_real - near_real * far_imag, axis=2)
    factor = band_scale / (
        2.0 * COMP * K * jnp.sqrt((near_energy + EPSILON) * (far_energy + EPSILON))
    )
    cross = (jnp.concatenate([real_part, imag_part], axis=-1) * factor[..., None]).astype(
        jnp.bfloat16
    )
    lagged = jnp.dot(cross.reshape(-1, 2 * K), inverse, preferred_element_type=jnp.float32)
    return lagged.reshape(cross.shape[:-1] + (LAGS,)).astype(jnp.bfloat16)


def body(windows, pick_mask, band_member, event_owner, partners):
    arch_count = lax.axis_size("arch")
    clus_count = lax.axis_size("clus")
    device_count = arch_count * clus_count
    block_events = windows.shape[0]
    group_stations = windows.shape[1] // arch_count
    capacity = 2 * block_events // clus_count
    owner_slots = capacity * device_count
    event_total = event_owner.shape[0]
    arch_index = lax.axis_index("arch")
    clus_index = lax.axis_index("clus")
    source_index = arch_index * clus_count + clus_index
    forward = forward_table()
    inverse = inverse_table()
    slot_rows = slot_layout(event_owner, device_count, block_events, owner_slots, capacity)
    masked = windows * pick_mask[:, :, None, None].astype(jnp.bfloat16)
    width = masked.shape[-1]
    local_rows = lax.dynamic_slice_in_dim(slot_rows, source_index * block_events, block_events)
    local_owner = lax.dynamic_slice_in_dim(event_owner, source_index * block_events, block_events)
    local_rank = local_rows - local_owner * owner_slots - source_index * capacity
    send_slot = local_owner * capacity + local_rank
    send_count = clus_count * capacity
    selector = (jnp.arange(send_count, dtype=jnp.int32)[:, None] == send_slot[None, :]).astype(
        jnp.bfloat16
    )
    picked = jnp.dot(selector, masked.reshape(block_events, -1), preferred_element_type=jnp.float32)
    picked = picked.astype(jnp.bfloat16).reshape(
        send_count, arch_count, group_stations, COMP, width
    )
    outgoing = jnp.moveaxis(picked, 1, 0)
    outgoing = outgoing.reshape(arch_count, clus_count, capacity, group_stations, COMP, width)
    flat_out = outgoing.reshape(arch_count * clus_count, capacity, group_stations, COMP, width)
    received = lax.all_to_all(flat_out, ("arch", "clus"), split_axis=0, concat_axis=0, tiled=True)
    received = received.reshape(owner_slots, group_stations, COMP, width)
    spectra = transform(received, forward)
    energies = jnp.mean(jnp.square(spectra.astype(jnp.float32)), axis=(2, 3))
    following = from_behind(spectra, "clus", -1)
    following_energy = jnp.mean(jnp.square(following.astype(jnp.float32)), axis=(2, 3))
    stacked = jnp.concatenate([spectra, following], axis=0)
    stacked_flat = stacked.reshape(2 * owner_slots, -1)
    stacked_energy = jnp.concatenate([energies, following_energy], axis=0)
    local_slot = slot_rows - clus_index * owner_slots
    mine = event_owner == clus_index
    matches = (jnp.arange(owner_slots, dtype=jnp.int32)[:, None] == local_slot[None, :]) & mine[
        None, :
    ]
    event_numbers = jnp.arange(event_total, dtype=jnp.int32) + 1
    slot_ids = jnp.sum(jnp.where(matches, event_numbers[None, :], 0), axis=1) - 1
    safe_ids = jnp.maximum(slot_ids, 0)
    partner_ids = jnp.take(partners, safe_ids, axis=0)
    partner_owner = jnp.take(event_owner, partner_ids)
    partner_row = jnp.take(slot_rows, partner_ids) - partner_owner * owner_slots
    lookup = jnp.where(partner_owner == clus_index, 0, owner_slots) + partner_row
    band_scale = lax.dynamic_slice_in_dim(
        band_member, arch_index * group_stations, group_stations
    ).astype(jnp.float32)
    candidates = jnp.arange(2 * owner_slots, dtype=jnp.int32)

    def one_column(column):
        chosen = column[:, None] == candidates[None, :]
        far = jnp.dot(chosen.astype(jnp.bfloat16), stacked_flat, preferred_element_type=jnp.float32)
        far = far.astype(jnp.bfloat16).reshape(spectra.shape)
        far_energy = jnp.dot(
            chosen.astype(jnp.float32), stacked_energy, precision=lax.Precision.HIGHEST
        )
        return correlate(spectra, far, energies, far_energy, band_scale, inverse)

    lagged = lax.map(one_column, lookup.T)
    return jnp.moveaxis(lagged, 0, 1)


def solution(mesh):
    return jax.shard_map(
        body,
        mesh=mesh,
        in_specs=(P(("arch", "clus"), None, None, None), P(("arch", "clus"), None), P(), P(), P()),
        out_specs=P("clus", None, "arch", None),
        check_vma=False,
    )
```

profile of v0, /device:TPU:1, one launch (start us, length us, event | category | flops | bytes accessed | tf_op | source)
XLA Modules:
  0.0 449.3 jit_solution(1214885345998223008)
XLA Ops:
  5.3 3.0 reshape.119
  10.5 7.0 %reshape.120 = bf16[64,4,4,3,400]{4,3,2,1,0:T(4,128)(2,1)} reshape(bf16[64,19200]{1,0:T(8,128)(2,1)S(1)} %convolution_convert_fusion.2) | data formatting | bytes 4915200 | tf_op jit(solution)/shard_map/reshape | solution.py:103
  17.5 5.5 %copy.64 = bf16[4,64,4,3,400]{4,2,3,1,0:T(4,128)(2,1)} copy(bf16[4,64,4,3,400]{4,3,2,0,1:T(4,128)(2,1)} %bitcast.30) | data formatting | bytes 4915200 | tf_op jit(solution)/shard_map/transpose | solution.py:106
  23.0 11.5 %all-to-all-start = ((bf16[128,2,4,3,400]{4,2,3,1,0:T(4,128)(2,1)}), bf16[128,2,4,3,400]{4,2,3,1,0:T(4,128)(2,1)S(1)}, u32[]{:S(2)}, u32[]{:S(2)}) async-start(bf16[128,2,4,3,400]{4,2,3,1,0:T(4,128)(2,1)} %bitcast.31), calls=%async_computation | async-start | bytes 6291456 | tf_op jit(solution)/shard_map/all_to_all | solution.py:109
  34.5 3.0 copy.66
  42.1 33.8 %all-to-all-done = bf16[128,2,4,3,400]{4,2,3,1,0:T(4,128)(2,1)S(1)} async-done(((bf16[128,2,4,3,400]{4,2,3,1,0:T(4,128)(2,1)}), bf16[128,2,4,3,400]{4,2,3,1,0:T(4,128)(2,1)S(1)}, u32[]{:S(2)}, u32[]{:S(2)}) %all-to-all-start) | async-done | bytes 2457632 | tf_op jit(solution)/shard_map/all_to_all | solution.py:109
  75.9 4.9 %copy.65 = bf16[128,2,4,3,400]{4,3,2,1,0:T(4,128)(2,1)} copy(bf16[128,2,4,3,400]{4,2,3,1,0:T(4,128)(2,1)S(1)} %all-to-all-done) | data formatting | bytes 4915200 | tf_op jit(solution)/shard_map/all_to_all | solution.py:109
  80.9 7.5 %reshape_reshape.7 = bf16[3072,400]{1,0:T(8,128)(2,1)S(1)} reshape(bf16[128,2,4,3,400]{4,3,2,1,0:T(4,128)(2,1)} %copy.65) | data formatting | bytes 4915200 | tf_op jit(solution)/shard_map/reshape;reshape | solution.py:45
  90.5 4.0 reshape.121
  97.8 45.5 %gather_fusion.2 = s32[8192]{0:T(1024)S(1)} fusion(s32[4096]{0:T(1024)S(1)} %get-tuple-element.145, s32[8192]{0:T(1024)S(1)} %broadcast_clamp_fusion), kind=kCustom, calls=%fused_computation.1.clone | custom fusion | bytes 98304 | tf_op jit(solution)/shard_map/jit(_take)/gather | solution.py:128
  143.4 45.5 %gather_fusion.1 = s32[8192]{0:T(1024)S(1)} fusion(s32[4096]{0:T(1024)S(1)} %copy-done, s32[8192]{0:T(1024)S(1)} %broadcast_clamp_fusion), kind=kCustom, calls=%fused_computation.clone | custom fusion | bytes 98304 | tf_op jit(solution)/shard_map/jit(_take)/gather | solution.py:127
  189.8 4.3 concatenate.25
  206.4 3.1 copy.75
  209.4 239.8 %while.11 = (s32[]{:T(128)}, bf16[32,256,4,128]{3,2,0,1:T(4,128)(2,1)}, bf16[256,4,3,256]{0,3,2,1:T(8,128)(2,1)}, s32[32,256]{1,0:T(8,128)S(1)}, bf16[512,3072]{...) while((s32[]{:T(128)}, ...), condition=%wide.region_8.10_spmd.clone, body=%wide.region_5.9_spmd.clone.sunk | while | flops 885134336 | bytes 13984377 | solution.py:144
  209.4 2.9 convolution_convert_fusion.5
  216.9 2.9 convolution_convert_fusion.5
  224.4 2.9 convolution_convert_fusion.5
  231.9 2.9 convolution_convert_fusion.5
  239.4 2.9 convolution_convert_fusion.5
  246.9 2.9 convolution_convert_fusion.5
  254.4 2.9 convolution_convert_fusion.5
  261.9 2.9 convolution_convert_fusion.5
  269.4 2.9 convolution_convert_fusion.5
  276.9 2.9 convolution_convert_fusion.5
  284.4 2.9 convolution_convert_fusion.5
  291.9 2.9 convolution_convert_fusion.5
  314.4 2.9 convolution_convert_fusion.5
  321.9 2.9 convolution_convert_fusion.5
  359.3 2.9 convolution_convert_fusion.5
  366.8 2.9 convolution_convert_fusion.5
  411.8 2.9 convolution_convert_fusion.5
  419.3 2.9 convolution_convert_fusion.5
  (265 shorter events, 216.9 us)
Async XLA Ops:
  5.3 3.0 copy-start
  23.0 52.9 %all-to-all-start = ((bf16[128,2,4,3,400]{4,2,3,1,0:T(4,128)(2,1)}), bf16[128,2,4,3,400]{4,2,3,1,0:T(4,128)(2,1)S(1)}, u32[]{:S(2)}, u32[]{:S(2)}) async-start(bf16[128,2,4,3,400]{4,2,3,1,0:T(4,128)(2,1)} %bitcast.31), calls=%async_computation | async-start | bytes 6291456 | tf_op jit(solution)/shard_map/all_to_all | solution.py:109
  96.3 103.3 %collective-permute-start = (bf16[256,4,3,256]{3,0,2,1:T(8,128)(2,1)}, bf16[256,4,3,256]{3,0,2,1:T(8,128)(2,1)}, u32[]{:S(2)}, u32[]{:S(2)}) collective-permute-start(bf16[256,4,3,256]{3,0,2,1:T(8,128)(2,1)} %copy.67), channel_id=1, source_target_pairs={{1,0},{2,1},{3,2},{4,3},{5,4},{6,5},{7,6},{8,7},{9,8},{10,9},{11,1... | collective-permute-start | bytes 4718600 | tf_op jit(solution)/shard_map/ppermute | solution.py:21
  143.4 46.0 %copy-start.2 = (s32[16]{0:T(128)S(1)}, s32[16]{0:T(128)}, u32[]{:S(2)}) copy-start(s32[16]{0:T(128)} %param.11) | copy-start | bytes 196
  196.6 1.4 copy-start.1
where the time goes:
time: 452 us; the launch traced here: 449 us
  local copies, waits for them, and re-layouts  200 us (44%)
  matrix products  122 us (27%)
  other arithmetic  79 us (17%)
  waiting for transfers between devices  33.8 us (7%)
  starting transfers between devices  12.8 us (3%)
    dot_general x32, matrix products, one_column(): jnp.dot(chosen.astype(jnp.bfloat16), stacked_flat, preferred_element_type...  93.1 us
    reduce_sum x32, other arithmetic, correlate(): real_part = jnp.sum(near_real * far_real + near_imag * far_imag, axis=2)  69.1 us
    gather x2, local copies, waits for them, and re-layouts, body(): partner_owner = jnp.take(event_owner, partner_ids)  45.6 us
    gather x2, local copies, waits for them, and re-layouts, body(): partner_row = jnp.take(slot_rows, partner_ids) - partner_owner * owner_slots  45.6 us
    all_to_all x1, waiting for transfers between devices, body(): lax.all_to_all(flat_out, ('arch', 'clus'), split_axis=0, concat_axis=0, t...  33.8 us
    dynamic_update_slice x32, local copies, waits for them, and re-layouts, body(): lagged = lax.map(one_column, lookup.T)  29.2 us
    convert_element_type x32, local copies, waits for them, and re-layouts, one_column(): far = far.astype(jnp.bfloat16).reshape(spectra.shape)  22.3 us
    dot_general x32, matrix products, one_column(): jnp.dot(chosen.astype(jnp.float32), stacked_energy, precision=lax.Precisi...  13.3 us
  transfers between devices with their start and end apart: 2, of which 1 were waited for; matrix products, arithmetic and copies ran while one was open for 24% of the time, Pallas kernels for 0%

commit v1 on v0

v1 whole, which is shorter than its diff:
```python
import functools
import math

import jax
import jax.numpy as jnp
import numpy as np
from jax import lax
from jax.experimental import pallas as pl
from jax.experimental.pallas import tpu as pltpu
from jax.sharding import PartitionSpec as P

L = 400
COMP = 3
K = 128
K0 = 16
LAGS = 128
EPSILON = 1e-06

EVENTS = 4096
BLOCK = 32
NB = 32
CAP = 2
STATIONS = 16
GROUP = 4
ROWS = COMP * GROUP * 2
TILE = GROUP * 2
PER_STEP = 8


def forward_table():
    samples = np.arange(L, dtype=np.int32)
    bins = np.arange(K, dtype=np.int32) + K0
    turns = samples[:, None] * bins[None, :] % (2 * L)
    phase = turns.astype(np.float32) * np.float32(math.pi / L)
    taper = np.float32(0.5) - np.float32(0.5) * np.cos(
        (samples.astype(np.float32) + np.float32(0.5)) * np.float32(2.0 * math.pi / L)
    )
    table = np.concatenate(
        [taper[:, None] * np.cos(phase), -taper[:, None] * np.sin(phase)], axis=1
    )
    return table.astype(jnp.bfloat16)


def inverse_table():
    bins = np.arange(K, dtype=np.int32) + K0
    shifts = np.arange(LAGS, dtype=np.int32) - LAGS // 2
    turns = np.remainder(bins[:, None] * shifts[None, :], 2 * L)
    phase = turns.astype(np.float32) * np.float32(math.pi / L)
    return np.concatenate([np.cos(phase), -np.sin(phase)], axis=0).astype(jnp.bfloat16)


def prepare_kernel(owner_ref, windows_ref, mask_ref, table_ref, out_ref, spectra, slots, counts):
    source = lax.axis_index("arch") * lax.axis_size("clus") + lax.axis_index("clus")
    owners = counts.shape[0]
    mask = mask_ref[...].astype(jnp.float32)
    table = table_ref[...]
    per = 4
    for chunk in range(BLOCK // per):
        rows = per * COMP * STATIONS
        spec = jnp.dot(
            windows_ref[chunk * rows : (chunk + 1) * rows, :],
            table,
            preferred_element_type=jnp.float32,
        )
        for e in range(per):
            event = chunk * per + e
            keep = jnp.broadcast_to(mask[:, event : event + 1], (STATIONS, K))
            for c in range(COMP):
                at = (e * COMP + c) * STATIONS
                to = (event * COMP + c) * STATIONS * 2
                spectra[pl.ds(to, STATIONS, stride=2), :] = spec[at : at + STATIONS, :K] * keep
                spectra[pl.ds(to + 1, STATIONS, stride=2), :] = spec[at : at + STATIONS, K:] * keep

    for o in range(owners):
        counts[o] = 0
        slots[2 * o] = -1
        slots[2 * o + 1] = -1

    def place(e, carry):
        owner = owner_ref[source * BLOCK + e]
        rank = counts[owner]
        slots[owner * CAP + rank] = e
        counts[owner] = rank + 1
        return carry

    lax.fori_loop(0, BLOCK, place, 0)

    def fill(o, carry):
        parts = [[], [], [], []]
        for r in range(CAP):
            e = slots[o * CAP + r]
            valid = jnp.where(e >= 0, 1.0, 0.0).astype(jnp.float32)
            base = jnp.maximum(e, 0) * (COMP * STATIONS * 2)
            for c in range(COMP):
                for a in range(STATIONS // GROUP):
                    start = pl.multiple_of(base + c * STATIONS * 2 + a * TILE, TILE)
                    parts[a].append(spectra[pl.ds(start, TILE), :] * valid)
        for a in range(STATIONS // GROUP):
            out_ref[a * owners + o] = jnp.concatenate(parts[a], axis=0).astype(jnp.bfloat16)
        return carry

    lax.fori_loop(0, owners, fill, 0)


def index_kernel(owner_ref, partners_ref, out_ref):
    mine = lax.axis_index("clus")
    own = owner_ref[...]
    lane = lax.broadcasted_iota(jnp.int32, own.shape, 1)
    inside = lane % BLOCK
    rank = jnp.zeros(own.shape, jnp.int32)
    for d in range(1, BLOCK):
        same = (pltpu.roll(own, d, 1) == own) & (inside >= d)
        rank = rank + same.astype(jnp.int32)
    row = lax.broadcasted_iota(jnp.int32, own.shape, 0)
    rank_word = jnp.sum(rank << row, axis=0, keepdims=True)
    far_word = jnp.sum((own != mine).astype(jnp.int32) << row, axis=0, keepdims=True)
    total = jnp.zeros((2 * CAP * NB, 128), jnp.float32)
    shard_of_lane = lax.broadcasted_iota(jnp.int32, (128, 128), 0) // BLOCK
    shard = lax.broadcasted_iota(jnp.int32, (128, 128), 1)
    for t in range(own.shape[0]):
        p = partners_ref[:, t * 128 : (t + 1) * 128]
        high, low = p // 128, p % 128
        parts = []
        for r in range(CAP):
            take = (own[t : t + 1, :] == mine) & (rank[t : t + 1, :] == r)
            for half in (high, low):
                parts.append(jnp.where(take, half, 0).astype(jnp.float32))
        stacked = jnp.concatenate(parts, axis=0).astype(jnp.bfloat16)
        spread = (shard_of_lane + t * (128 // BLOCK) == shard).astype(jnp.float32)
        total = total + jnp.dot(
            stacked, spread.astype(jnp.bfloat16), preferred_element_type=jnp.float32
        )
    for r in range(CAP):
        high = total[2 * r * NB : (2 * r + 1) * NB].astype(jnp.int32)
        low = total[(2 * r + 1) * NB : (2 * r + 2) * NB].astype(jnp.int32)
        rank_bits = jnp.take_along_axis(jnp.broadcast_to(rank_word, low.shape), low, axis=1)
        far_bits = jnp.take_along_axis(jnp.broadcast_to(far_word, low.shape), low, axis=1)
        rank_bit = lax.shift_right_logical(rank_bits, high) & 1
        far_bit = lax.shift_right_logical(far_bits, high) & 1
        source = high * (128 // BLOCK) + low // BLOCK
        slot = far_bit * 256 + source * CAP + rank_bit
        out_ref[r * NB : (r + 1) * NB, :] = slot


def correlate_kernel(lookup, band_ref, near_ref, far_ref, lag_ref, out_ref, table, cross_a, cross_b):
    step = pl.program_id(0)
    row = lax.broadcasted_iota(jnp.int32, (TILE, 128), 0)
    even = row % 2 == 0

    @pl.when(step == 0)
    def _():
        def normalize(ref, first):
            def one(i, carry):
                start = pl.multiple_of(i * (2 * ROWS), 2 * ROWS)
                block = ref[pl.ds(start, 2 * ROWS), :].astype(jnp.float32)
                for e in range(2):
                    parts = [
                        block[e * ROWS + c * TILE : e * ROWS + (c + 1) * TILE] for c in range(COMP)
                    ]
                    power = parts[0] * parts[0] + parts[1] * parts[1] + parts[2] * parts[2]
                    power = power + jnp.where(
                        even, pltpu.roll(power, TILE - 1, 0), pltpu.roll(power, 1, 0)
                    )
                    energy = jnp.sum(power, axis=1, keepdims=True) * (1.0 / (COMP * 2 * K))
                    scale = lax.rsqrt(energy + EPSILON)
                    for c in range(COMP):
                        to = pl.multiple_of(
                            first * ROWS + start + e * ROWS + c * TILE, TILE
                        )
                        table[pl.ds(to, TILE), :] = parts[c] * scale
                return carry

            lax.fori_loop(0, ref.shape[0] // (2 * ROWS), one, 0, unroll=4)

        normalize(near_ref, 0)
        normalize(far_ref, 256)

    band = jnp.zeros((TILE, 128), jnp.float32)
    first = lax.axis_index("arch") * GROUP
    for s in range(GROUP):
        member = band_ref[first + s].astype(jnp.float32) * (1.0 / (2.0 * COMP * K))
        band = jnp.where(row // 2 == s, member, band)
    lag = lag_ref[...]
    for i in range(PER_STEP):
        slot = step * PER_STEP + i
        shard = step * (PER_STEP // CAP) + i // CAP
        direct, turned = [], []
        for c in range(COMP):
            at = pl.multiple_of(slot * ROWS + c * TILE, TILE)
            piece = table[pl.ds(at, TILE), :] * band
            direct.append(piece)
            turned.append(
                jnp.where(even, pltpu.roll(piece, TILE - 1, 0), -pltpu.roll(piece, 1, 0))
            )
        for j in range(NB):
            base = lookup[(i % CAP) * NB + j, shard] * ROWS
            v = [table[pl.ds(pl.multiple_of(base + c * TILE, TILE), TILE), :] for c in range(COMP)]
            to = (i * NB + j) * TILE
            cross_a[to : to + TILE, :] = direct[0] * v[0] + direct[1] * v[1] + direct[2] * v[2]
            cross_b[to : to + TILE, :] = turned[0] * v[0] + turned[1] * v[1] + turned[2] * v[2]
        rows = NB * GROUP
        at = i * NB * TILE
        real = cross_a[pl.ds(at, rows, stride=2), :] + cross_a[pl.ds(at + 1, rows, stride=2), :]
        imag = cross_b[pl.ds(at, rows, stride=2), :] + cross_b[pl.ds(at + 1, rows, stride=2), :]
        cross = jnp.concatenate([real, imag], axis=1).astype(jnp.bfloat16)
        lagged = jnp.dot(cross, lag, preferred_element_type=jnp.float32)
        out_ref[i * rows : (i + 1) * rows, :] = lagged.astype(jnp.bfloat16)


def body(windows, pick_mask, band_member, event_owner, partners):
    arch_count = lax.axis_size("arch")
    clus_count = lax.axis_size("clus")
    device_count = arch_count * clus_count
    vmem = pl.BlockSpec(memory_space=pltpu.VMEM)
    smem = pl.BlockSpec(memory_space=pltpu.SMEM)
    limit = 48 * 1024 * 1024

    rows = BLOCK * COMP * STATIONS
    outgoing = pl.pallas_call(
        prepare_kernel,
        out_shape=jax.ShapeDtypeStruct((device_count, CAP * ROWS, 128), jnp.bfloat16),
        in_specs=[smem, vmem, vmem, vmem],
        out_specs=vmem,
        scratch_shapes=[
            pltpu.VMEM((rows * 2, K), jnp.float32),
            pltpu.SMEM((clus_count * CAP,), jnp.int32),
            pltpu.SMEM((clus_count,), jnp.int32),
        ],
        compiler_params=pltpu.CompilerParams(vmem_limit_bytes=limit),
        name="prepare",
    )(
        event_owner,
        jnp.transpose(windows, (0, 2, 1, 3)).reshape(rows, L),
        pick_mask.T,
        jnp.asarray(forward_table()),
    )
    lookup = pl.pallas_call(
        index_kernel,
        out_shape=jax.ShapeDtypeStruct((CAP * NB, device_count), jnp.int32),
        in_specs=[vmem, vmem],
        out_specs=vmem,
        compiler_params=pltpu.CompilerParams(vmem_limit_bytes=limit),
        name="lookup",
    )(event_owner.reshape(EVENTS // 128, 128), partners.T)

    received = lax.all_to_all(outgoing, ("arch", "clus"), split_axis=0, concat_axis=0, tiled=True)
    near = received.reshape(device_count * CAP * ROWS, 128)
    route = [((i + 1) % clus_count, i) for i in range(clus_count)]
    far = lax.ppermute(near, "clus", route)

    slots = device_count * CAP
    pair_rows = slots * NB * GROUP
    block_rows = PER_STEP * NB * GROUP
    result = pl.pallas_call(
        correlate_kernel,
        out_shape=jax.ShapeDtypeStruct((pair_rows, LAGS), jnp.bfloat16),
        grid=(slots // PER_STEP,),
        in_specs=[smem, smem, vmem, vmem, vmem],
        out_specs=pl.BlockSpec((block_rows, LAGS), lambda i: (i, 0)),
        scratch_shapes=[
            pltpu.VMEM((2 * slots * ROWS, 128), jnp.float32),
            pltpu.VMEM((PER_STEP * NB * TILE, 128), jnp.float32),
            pltpu.VMEM((PER_STEP * NB * TILE, 128), jnp.float32),
        ],
        compiler_params=pltpu.CompilerParams(vmem_limit_bytes=limit),
        name="correlate",
    )(lookup, band_member, near, far, jnp.asarray(inverse_table()))
    return result.reshape(slots, NB, GROUP, LAGS)


def solution(mesh):
    return jax.shard_map(
        body,
        mesh=mesh,
        in_specs=(P(("arch", "clus"), None, None, None), P(("arch", "clus"), None), P(), P(), P()),
        out_specs=P("clus", None, "arch", None),
        check_vma=False,
    )
```

time: 452 us -> 95.9 us (0.21)
  local copies, waits for them, and re-layouts: 200 us -> 3.77 us
  matrix products: 122 us -> 0 us
  other arithmetic: 79 us -> 0 us
  Pallas kernels: 0 us -> 37.1 us
  blocking collectives: 0 us -> 36 us
  waiting for transfers between devices: 33.8 us -> 17.5 us
  starting transfers between devices: 12.8 us -> 1.24 us
    dot_general x98 -> x0, matrix products: 122 us -> none  [the longest x32 93.1 us: one_column(): jnp.dot(chosen.astype(jnp.bfloat16), stacked_flat, preferred_element_type...]
    gather x5 -> x0, local copies, waits for them, and re-layouts: 93.5 us -> none  [the longest x2 45.6 us: body(): partner_owner = jnp.take(event_owner, partner_ids)]
    reduce_sum x36 -> x0, other arithmetic: 72.7 us -> none  [the longest x32 69.1 us: correlate(): real_part = jnp.sum(near_real * far_real + near_imag * far_imag, axis=2)]
    pallas_call x0 -> x3, Pallas kernels: none -> 37.1 us  [the longest x1 33.7 us: body(): pl.pallas_call(correlate_kernel, out_shape=jax.ShapeDtypeStruct((pair_row...]
    all_to_all x0 -> x1, blocking collectives: none -> 36 us  [body(): lax.all_to_all(outgoing, ('arch', 'clus'), split_axis=0, concat_axis=0, t...]
    all_to_all x1 -> x0, waiting for transfers between devices: 33.8 us -> none  [body(): lax.all_to_all(flat_out, ('arch', 'clus'), split_axis=0, concat_axis=0, t...]
    dynamic_update_slice x32 -> x0, local copies, waits for them, and re-layouts: 29.2 us -> none  [body(): lagged = lax.map(one_column, lookup.T)]
    convert_element_type x33 -> x0, local copies, waits for them, and re-layouts: 22.4 us -> none  [the longest x32 22.3 us: one_column(): far = far.astype(jnp.bfloat16).reshape(spectra.shape)]
  transfers between devices with their start and end apart: 2 -> 1, of which waited for: 1 -> 1; matrix products, arithmetic and copies ran while one was open for 24% -> 0% of each run, Pallas kernels for 0% -> 1%
where the time goes in v1:
time: 95.9 us; the launch traced here: 95.7 us
  Pallas kernels  37.1 us (39%)
  blocking collectives  36 us (38%)
  waiting for transfers between devices  17.5 us (18%)
  local copies, waits for them, and re-layouts  3.77 us (4%)
  starting transfers between devices  1.24 us (1%)
    all_to_all x1, blocking collectives, body(): lax.all_to_all(outgoing, ('arch', 'clus'), split_axis=0, concat_axis=0, t...  36 us
    pallas_call x1, Pallas kernels, body(): pl.pallas_call(correlate_kernel, out_shape=jax.ShapeDtypeStruct((pair_row...  33.7 us
    ppermute x1, waiting for transfers between devices, body(): far = lax.ppermute(near, 'clus', route)  17.5 us
    unnamed x14, local copies, waits for them, and re-layouts  3.77 us
    pallas_call x1, Pallas kernels, body(): pl.pallas_call(prepare_kernel, out_shape=jax.ShapeDtypeStruct((device_cou...  2.36 us
  transfers between devices with their start and end apart: 1, of which 1 were waited for; matrix products, arithmetic and copies ran while one was open for 0% of the time, Pallas kernels for 1%

profile of v1, /device:TPU:1, one launch (start us, length us, event | category | flops | bytes accessed | tf_op | source)
XLA Modules:
  0.0 95.7 jit_solution(600961037970842111)
XLA Ops:
  0.0 0.0 copy-start
  0.0 1.4 %copy-done = bf16[32,16,3,400]{3,1,2,0:T(8,128)(2,1)S(1)} copy-done((bf16[32,16,3,400]{3,1,2,0:T(8,128)(2,1)S(1)}, bf16[32,16,3,400]{3,1,2,0:T(8,128)(2,1)}, u32[]{:S(2)}) %copy-start) | copy-done | bytes 1228824
  1.4 0.0 copy-start.2
  1.4 0.9 copy-done.2
  2.3 0.0 copy-start.4
  2.3 0.7 copy-done.4
  3.1 0.0 copy-start.5
  3.1 0.7 copy-done.5
  3.8 2.4 %prepare.1 = bf16[128,48,128]{2,1,0:T(8,128)(2,1)S(1)} custom-call(s32[4096]{0:T(1024)S(1)} %copy-done.4, bf16[1536,400]{1,0:T(8,128)(2,1)S(1)} %bitcast.10, s32[16,32]{1,0:T(8,128)S(1)} %bitcast.13, bf16[400,256]{1,0:T(8,128)(2,1)S(1)} %copy-done.2), custom_call_target="tpu_custom_call" | custom-call | tf_op jit(solution)/shard_map/prepare/pallas_call | solution.py:219
  6.1 0.0 copy-start.1
  6.1 0.0 copy-start.3
  6.2 0.0 copy-start.6
  6.2 36.0 %all_to_all.5 = bf16[128,48,128]{2,1,0:T(8,128)(2,1)S(1)} all-to-all(bf16[128,48,128]{2,1,0:T(8,128)(2,1)S(1)} %prepare.1), channel_id=1, replica_groups=mesh['arch'=4,'clus'=32] {'arch','clus'}, dimensions={0} | all-to-all | bytes 3145728 | tf_op jit(solution)/shard_map/all_to_all | solution.py:246
  42.2 1.2 %collective-permute-start = (bf16[6144,128]{1,0:T(8,128)(2,1)S(1)}, bf16[6144,128]{1,0:T(8,128)(2,1)S(1)}, u32[]{:S(2)}, u32[]{:S(2)}) collective-permute-start(bf16[6144,128]{1,0:T(8,128)(2,1)S(1)} %bitcast.8), channel_id=1, source_target_pairs={{1,0},{2,1},{3,2},{4,3},{5,4},{6,5},{7,6},{8,7},{9,8},{10,9},{11,1... | collective-permute-start | bytes 4718600 | tf_op jit(solution)/shard_map/ppermute | solution.py:249
  43.4 0.0 copy-done.1
  43.4 1.1 %lookup.1 = s32[64,128]{1,0:T(8,128)S(1)} custom-call(s32[32,128]{1,0:T(8,128)S(1)} %bitcast.12, s32[32,4096]{1,0:T(8,128)S(1)} %bitcast.11), custom_call_target="tpu_custom_call" | custom-call | tf_op jit(solution)/shard_map/lookup/pallas_call | solution.py:237
  44.5 17.5 %collective-permute-done.far_ref = bf16[6144,128]{1,0:T(8,128)(2,1)S(1)} collective-permute-done((bf16[6144,128]{1,0:T(8,128)(2,1)S(1)}, bf16[6144,128]{1,0:T(8,128)(2,1)S(1)}, u32[]{:S(2)}, u32[]{:S(2)}) %collective-permute-start) | collective-permute-done | bytes 1572896 | tf_op jit(solution)/shard_map/ppermute | solution.py:249
  62.0 0.0 copy-done.3
  62.0 0.0 copy-done.6
  62.0 33.7 %correlate.1 = bf16[32768,128]{1,0:T(8,128)(2,1)} custom-call(s32[64,128]{1,0:T(8,128)S(1)} %lookup.1, s32[16]{0:T(128)S(1)} %copy-done.6, bf16[6144,128]{1,0:T(8,128)(2,1)S(1)} %bitcast.9, bf16[6144,128]{1,0:T(8,128)(2,1)S(1)} %collective-permute-done.far_ref, bf16[256,128]{1,0:T(8,128)(2,1)S(1)} %copy-done.3), custom_call_target="tpu_custom_call" | custom-call | tf_op jit(solution)/shard_map/correlate/pallas_call | solution.py:254
Async XLA Ops:
  0.0 1.4 %copy-start = (bf16[32,16,3,400]{3,1,2,0:T(8,128)(2,1)S(1)}, bf16[32,16,3,400]{3,1,2,0:T(8,128)(2,1)}, u32[]{:S(2)}) copy-start(bf16[32,16,3,400]{3,1,2,0:T(8,128)(2,1)} %param.7) | copy-start | bytes 3686404
  1.4 0.9 copy-start.2
  2.3 0.7 copy-start.4
  3.1 0.7 copy-start.5
  6.1 37.3 %copy-start.1 = (s32[4096,32]{0,1:T(8,128)S(1)}, s32[4096,32]{0,1:T(8,128)}, u32[]{:S(2)}) copy-start(s32[4096,32]{0,1:T(8,128)} %param.11) | copy-start | bytes 1572868
  6.1 55.9 %copy-start.3 = (bf16[256,128]{1,0:T(8,128)(2,1)S(1)}, bf16[256,128]{1,0:T(8,128)(2,1)}, u32[]{:S(2)}) copy-start(bf16[256,128]{1,0:T(8,128)(2,1)} %constant.5.clone.lag_ref) | copy-start | bytes 196612
  6.2 55.9 %copy-start.6 = (s32[16]{0:T(128)S(1)}, s32[16]{0:T(128)}, u32[]{:S(2)}) copy-start(s32[16]{0:T(128)} %band_ref.1) | copy-start | bytes 196
  42.2 19.8 %collective-permute-start = (bf16[6144,128]{1,0:T(8,128)(2,1)S(1)}, bf16[6144,128]{1,0:T(8,128)(2,1)S(1)}, u32[]{:S(2)}, u32[]{:S(2)}) collective-permute-start(bf16[6144,128]{1,0:T(8,128)(2,1)S(1)} %bitcast.8), channel_id=1, source_target_pairs={{1,0},{2,1},{3,2},{4,3},{5,4},{6,5},{7,6},{8,7},{9,8},{10,9},{11,1... | collective-permute-start | bytes 4718600 | tf_op jit(solution)/shard_map/ppermute | solution.py:249

commit v2 on v1

--- a/solution.py
+++ b/solution.py
@@ -24,6 +24,7 @@
 GROUP = 4
 ROWS = COMP * GROUP * 2
 TILE = GROUP * 2
+PER_DOT = 4
 PER_STEP = 8
 
 
@@ -47,6 +48,11 @@
     turns = np.remainder(bins[:, None] * shifts[None, :], 2 * L)
     phase = turns.astype(np.float32) * np.float32(math.pi / L)
     return np.concatenate([np.cos(phase), -np.sin(phase)], axis=0).astype(jnp.bfloat16)
+
+
+def position(shard):
+    y, x, z, core = shard // 32, shard // 8 % 4, shard // 2 % 4, shard % 2
+    return ((z * 4 + y) * 4 + x) * 2 + core
 
 
 def prepare_kernel(owner_ref, windows_ref, mask_ref, table_ref, out_ref, spectra, slots, counts):
@@ -68,8 +74,12 @@
             for c in range(COMP):
                 at = (e * COMP + c) * STATIONS
                 to = (event * COMP + c) * STATIONS * 2
-                spectra[pl.ds(to, STATIONS, stride=2), :] = spec[at : at + STATIONS, :K] * keep
-                spectra[pl.ds(to + 1, STATIONS, stride=2), :] = spec[at : at + STATIONS, K:] * keep
+                real = spec[at : at + STATIONS, :K] * keep
+                imag = spec[at : at + STATIONS, K:] * keep
+                for a in range(STATIONS // GROUP):
+                    some = slice(a * GROUP, (a + 1) * GROUP)
+                    spectra[to + a * TILE : to + a * TILE + GROUP, :] = real[some]
+                    spectra[to + a * TILE + GROUP : to + (a + 1) * TILE, :] = imag[some]
 
     for o in range(owners):
         counts[o] = 0
@@ -138,14 +148,109 @@
         rank_bit = lax.shift_right_logical(rank_bits, high) & 1
         far_bit = lax.shift_right_logical(far_bits, high) & 1
         source = high * (128 // BLOCK) + low // BLOCK
-        slot = far_bit * 256 + source * CAP + rank_bit
-        out_ref[r * NB : (r + 1) * NB, :] = slot
-
-
-def correlate_kernel(lookup, band_ref, near_ref, far_ref, lag_ref, out_ref, table, cross_a, cross_b):
+        slot = far_bit * 256 + position(source) * CAP + rank_bit
+        out_ref[r * NB : (r + 1) * NB, :] = slot * ROWS
+
+
+MESH = pl.DeviceIdType.MESH
+GROUPS = [(2, 2), (2, 1), (1, 2), (2, 3), (3, 2), (1, 1), (3, 3), (1, 3), (3, 1), (2, 0), (0, 2), (1, 0), (0, 1), (3, 0), (0, 3), (0, 0)]
+SHARE = 8
+
+def exchange_kernel(out_ref, own_ref, next_ref, send_sem, extra_sem, own_sem, next_sem, to_next_sem, to_own_sem, from_own_sem, from_next_sem):
+    y = lax.axis_index("arch")
+    me = lax.axis_index("clus")
+    clus = lax.axis_size("clus")
+    arch = lax.axis_size("arch")
+    x, z, core = me // 8, me // 2 % 4, me % 2
+    before, after = lax.rem(me + clus - 1, clus), lax.rem(me + 1, clus)
+    after_z = after // 2 % 4
+    after_single = x * 8 + lax.rem(z + 1, 4) * 2
+    here = ((z * arch + y) * 4 + x) * 2 + core
+
+    barrier = pltpu.get_barrier_semaphore()
+
+    def greet(i, carry):
+        other = lax.rem(y * clus + me + i, arch * clus)
+        pl.semaphore_signal(barrier, inc=1, device_id=(other // clus, lax.rem(other, clus)), device_id_type=MESH)
+        return carry
+
+    lax.fori_loop(1, arch * clus, greet, 0)
+    pl.semaphore_wait(barrier, arch * clus - 1)
+
+    for dz, dy in GROUPS:
+        stays = dz in (0, 3)
+        buffer, sems = (own_ref, own_sem) if stays else (next_ref, next_sem)
+        sem = sems.at[((0 if dz == 0 else 1) if stays else dz - 1) * 4 + dy]
+        to_y, to_z = lax.rem(y + dy, arch), lax.rem(z + dz, 4)
+
+        def send(m, carry, dz=dz, dy=dy, stays=stays, buffer=buffer, sem=sem, to_y=to_y, to_z=to_z):
+            owner = lax.rem(x + m // 2, 4) * 8 + to_z * 2 + m % 2
+            target = owner if stays else lax.rem(owner + clus - 1, clus)
+            source = out_ref.at[to_y * clus + owner]
+
+            def remote(done):
+                pltpu.make_async_remote_copy(source, buffer.at[here], done, sem, device_id=(to_y, target), device_id_type=MESH).start()
+
+            if dy == 0 and dz == 0:
+                @pl.when(target == me)
+                def _():
+                    pltpu.make_async_copy(source, buffer.at[here], sem).start()
+
+                @pl.when(target != me)
+                def _():
+                    remote(send_sem)
+            elif dy == 0 and dz == 1:
+                @pl.when(target == me)
+                def _():
+                    pltpu.make_async_copy(source, buffer.at[here], sem).start()
+
+                single = (core == 0) & (owner == after_single)
+
+                @pl.when((target != me) & single)
+                def _():
+                    remote(extra_sem)
+
+                @pl.when((target != me) & jnp.logical_not(single))
+                def _():
+                    remote(send_sem)
+            else:
+                remote(send_sem)
+            return carry
+
+        lax.fori_loop(0, SHARE, send, 0)
+
+    forwards = []
+    for dz, dy in GROUPS:
+        from_y = lax.rem(y - dy + arch, arch)
+        if dz in (0, 3):
+            k = (0 if dz == 0 else 1) * 4 + dy
+            at = (lax.rem(z - dz + 4, 4) * arch + from_y) * SHARE
+            block = own_ref.at[pl.ds(at, SHARE)]
+            pltpu.make_async_copy(block, block, own_sem.at[k]).wait()
+            copy = pltpu.make_async_remote_copy(block, next_ref.at[pl.ds(at, SHARE)], to_next_sem.at[k], from_own_sem.at[k], device_id=(y, before), device_id_type=MESH)
+        else:
+            k = (dz - 1) * 4 + dy
+            at = (lax.rem(after_z - dz + 4, 4) * arch + from_y) * SHARE
+            block = next_ref.at[pl.ds(at, SHARE)]
+            pltpu.make_async_copy(block, block, next_sem.at[k]).wait()
+            copy = pltpu.make_async_remote_copy(block, own_ref.at[pl.ds(at, SHARE)], to_own_sem.at[k], from_next_sem.at[k], device_id=(y, after), device_id_type=MESH)
+        copy.start()
+        forwards.append(copy)
+    for copy in forwards:
+        copy.wait()
+    last = out_ref.at[pl.ds(0, arch * clus - 2)]
+    pltpu.make_async_copy(last, last, send_sem).wait()
+
+    @pl.when(core == 0)
+    def _():
+        one = out_ref.at[0]
+        pltpu.make_async_copy(one, one, extra_sem).wait()
+
+
+def correlate_kernel(lookup, band_ref, near_ref, far_ref, lag_ref, out_ref, table, *cross):
     step = pl.program_id(0)
     row = lax.broadcasted_iota(jnp.int32, (TILE, 128), 0)
-    even = row % 2 == 0
+    sign = jnp.where(row < GROUP, 1.0, -1.0).astype(jnp.float32)
 
     @pl.when(step == 0)
     def _():
@@ -158,19 +263,15 @@
                         block[e * ROWS + c * TILE : e * ROWS + (c + 1) * TILE] for c in range(COMP)
                     ]
                     power = parts[0] * parts[0] + parts[1] * parts[1] + parts[2] * parts[2]
-                    power = power + jnp.where(
-                        even, pltpu.roll(power, TILE - 1, 0), pltpu.roll(power, 1, 0)
-                    )
+                    power = power + pltpu.roll(power, GROUP, 0)
                     energy = jnp.sum(power, axis=1, keepdims=True) * (1.0 / (COMP * 2 * K))
                     scale = lax.rsqrt(energy + EPSILON)
                     for c in range(COMP):
-                        to = pl.multiple_of(
-                            first * ROWS + start + e * ROWS + c * TILE, TILE
-                        )
+                        to = pl.multiple_of(first * ROWS + start + e * ROWS + c * TILE, TILE)
                         table[pl.ds(to, TILE), :] = parts[c] * scale
                 return carry
 
-            lax.fori_loop(0, ref.shape[0] // (2 * ROWS), one, 0, unroll=4)
+            lax.fori_loop(0, ref.shape[0] // (2 * ROWS), one, 0, unroll=16)
 
         normalize(near_ref, 0)
         normalize(far_ref, 256)
@@ -179,32 +280,64 @@
     first = lax.axis_index("arch") * GROUP
     for s in range(GROUP):
         member = band_ref[first + s].astype(jnp.float32) * (1.0 / (2.0 * COMP * K))
-        band = jnp.where(row // 2 == s, member, band)
+        band = jnp.where(row % GROUP == s, member, band)
     lag = lag_ref[...]
-    for i in range(PER_STEP):
-        slot = step * PER_STEP + i
-        shard = step * (PER_STEP // CAP) + i // CAP
-        direct, turned = [], []
-        for c in range(COMP):
-            at = pl.multiple_of(slot * ROWS + c * TILE, TILE)
-            piece = table[pl.ds(at, TILE), :] * band
-            direct.append(piece)
-            turned.append(
-                jnp.where(even, pltpu.roll(piece, TILE - 1, 0), -pltpu.roll(piece, 1, 0))
-            )
-        for j in range(NB):
-            base = lookup[(i % CAP) * NB + j, shard] * ROWS
-            v = [table[pl.ds(pl.multiple_of(base + c * TILE, TILE), TILE), :] for c in range(COMP)]
-            to = (i * NB + j) * TILE
-            cross_a[to : to + TILE, :] = direct[0] * v[0] + direct[1] * v[1] + direct[2] * v[2]
-            cross_b[to : to + TILE, :] = turned[0] * v[0] + turned[1] * v[1] + turned[2] * v[2]
-        rows = NB * GROUP
-        at = i * NB * TILE
-        real = cross_a[pl.ds(at, rows, stride=2), :] + cross_a[pl.ds(at + 1, rows, stride=2), :]
-        imag = cross_b[pl.ds(at, rows, stride=2), :] + cross_b[pl.ds(at + 1, rows, stride=2), :]
-        cross = jnp.concatenate([real, imag], axis=1).astype(jnp.bfloat16)
-        lagged = jnp.dot(cross, lag, preferred_element_type=jnp.float32)
-        out_ref[i * rows : (i + 1) * rows, :] = lagged.astype(jnp.bfloat16)
+    rows = NB * GROUP
+    for i in range(0, PER_STEP, PER_DOT):
+        done = []
+        for d in range(PER_DOT):
+            shard = step * (PER_STEP // CAP) + (i + d) // CAP
+            real_r, real_i, imag_r, imag_i = [
+                ref.at[(i + d) * rows : (i + d + 1) * rows] for ref in cross
+            ]
+            near = position(shard) * CAP + (i + d) % CAP
+            direct, turned = [], []
+            for c in range(COMP):
+                at = pl.multiple_of(near * ROWS + c * TILE, TILE)
+                piece = table[pl.ds(at, TILE), :] * band
+                direct.append(piece)
+                turned.append(pltpu.roll(piece, GROUP, 0) * sign)
+            for j in range(NB):
+                base = lookup[((i + d) % CAP) * NB + j, shard]
+                v = [
+                    table[pl.ds(pl.multiple_of(base + c * TILE, TILE), TILE), :]
+                    for c in range(COMP)
+                ]
+                to = slice(j * GROUP, (j + 1) * GROUP)
+                both = direct[0] * v[0] + direct[1] * v[1] + direct[2] * v[2]
+                real_r[to, :] = both[:GROUP]
+                real_i[to, :] = both[GROUP:]
+                both = turned[0] * v[0] + turned[1] * v[1] + turned[2] * v[2]
+                imag_r[to, :] = both[:GROUP]
+                imag_i[to, :] = both[GROUP:]
+            real = real_r[...] + real_i[...]
+            imag = imag_r[...] + imag_i[...]
+            done.append(jnp.concatenate([real, imag], axis=1).astype(jnp.bfloat16))
+        lagged = jnp.dot(jnp.concatenate(done, axis=0), lag, preferred_element_type=jnp.float32)
+        out_ref[i * rows : (i + PER_DOT) * rows, :] = lagged.astype(jnp.bfloat16)
+
+
+def correlate_call(lookup, band_member, near, far):
+    vmem = pl.BlockSpec(memory_space=pltpu.VMEM)
+    smem = pl.BlockSpec(memory_space=pltpu.SMEM)
+    limit = 48 * 1024 * 1024
+    slots = near.shape[0] // ROWS
+    pair_rows = slots * NB * GROUP
+    block_rows = PER_STEP * NB * GROUP
+    result = pl.pallas_call(
+        correlate_kernel,
+        out_shape=jax.ShapeDtypeStruct((pair_rows, LAGS), jnp.bfloat16),
+        grid=(slots // PER_STEP,),
+        in_specs=[smem, smem, vmem, vmem, vmem],
+        out_specs=pl.BlockSpec((block_rows, LAGS), lambda i: (i, 0)),
+        scratch_shapes=[
+            pltpu.VMEM((2 * slots * ROWS, 128), jnp.float32),
+            *[pltpu.VMEM((block_rows, 128), jnp.float32) for _ in range(4)],
+        ],
+        compiler_params=pltpu.CompilerParams(vmem_limit_bytes=limit),
+        name="correlate",
+    )(lookup, band_member, near, far, jnp.asarray(inverse_table()))
+    return result.reshape(slots, NB, GROUP, LAGS)
 
 
 def body(windows, pick_mask, band_member, event_owner, partners):
@@ -243,29 +376,20 @@
         name="lookup",
     )(event_owner.reshape(EVENTS // 128, 128), partners.T)
 
-    received = lax.all_to_all(outgoing, ("arch", "clus"), split_axis=0, concat_axis=0, tiled=True)
-    near = received.reshape(device_count * CAP * ROWS, 128)
-    route = [((i + 1) % clus_count, i) for i in range(clus_count)]
-    far = lax.ppermute(near, "clus", route)
-
-    slots = device_count * CAP
-    pair_rows = slots * NB * GROUP
-    block_rows = PER_STEP * NB * GROUP
-    result = pl.pallas_call(
-        correlate_kernel,
-        out_shape=jax.ShapeDtypeStruct((pair_rows, LAGS), jnp.bfloat16),
-        grid=(slots // PER_STEP,),
-        in_specs=[smem, smem, vmem, vmem, vmem],
-        out_specs=pl.BlockSpec((block_rows, LAGS), lambda i: (i, 0)),
-        scratch_shapes=[
-            pltpu.VMEM((2 * slots * ROWS, 128), jnp.float32),
-            pltpu.VMEM((PER_STEP * NB * TILE, 128), jnp.float32),
-            pltpu.VMEM((PER_STEP * NB * TILE, 128), jnp.float32),
-        ],
-        compiler_params=pltpu.CompilerParams(vmem_limit_bytes=limit),
-        name="correlate",
-    )(lookup, band_member, near, far, jnp.asarray(inverse_table()))
-    return result.reshape(slots, NB, GROUP, LAGS)
+    own, following = pl.pallas_call(
+        exchange_kernel,
+        out_shape=[jax.ShapeDtypeStruct(outgoing.shape, outgoing.dtype)] * 2,
+        in_specs=[vmem],
+        out_specs=[vmem] * 2,
+        scratch_shapes=[pltpu.SemaphoreType.DMA] * 2 + [pltpu.SemaphoreType.DMA((8,))] * 6,
+        compiler_params=pltpu.CompilerParams(
+            collective_id=0, has_side_effects=True, vmem_limit_bytes=limit
+        ),
+        name="exchange",
+    )(outgoing)
+    near = own.reshape(device_count * CAP * ROWS, 128)
+    far = following.reshape(device_count * CAP * ROWS, 128)
+    return correlate_call(lookup, band_member, near, far)
 
 
 def solution(mesh):

time: 95.9 us -> 79.5 us (0.83)
  Pallas kernels: 37.1 us -> 74.3 us
  blocking collectives: 36 us -> 0 us
  waiting for transfers between devices: 17.5 us -> 0 us
  starting transfers between devices: 1.24 us -> 0 us
  local copies, waits for them, and re-layouts: 3.77 us -> 4.8 us
    pallas_call x1 -> x2, Pallas kernels: 33.7 us -> 70.9 us  [the longest x1 40.3 us: body(): pl.pallas_call(exchange_kernel, out_shape=[jax.ShapeDtypeStruct(outgoing....]
    all_to_all x1 -> x0, blocking collectives: 36 us -> none  [body(): lax.all_to_all(outgoing, ('arch', 'clus'), split_axis=0, concat_axis=0, t...]
    ppermute x1 -> x0, waiting for transfers between devices: 17.5 us -> none  [body(): far = lax.ppermute(near, 'clus', route)]
    ppermute x1 -> x0, starting transfers between devices: 1.24 us -> none  [body(): far = lax.ppermute(near, 'clus', route)]
    unnamed x14, local copies, waits for them, and re-layouts: 3.77 us -> 4.8 us
  transfers between devices with their start and end apart: 1 -> 0, of which waited for: 1 -> 0; matrix products, arithmetic and copies ran while one was open for 0% -> 0% of each run, Pallas kernels for 1% -> 0%
where the time goes in v2:
time: 79.5 us; the launch traced here: 79.2 us
  Pallas kernels  74.3 us (93%)
  local copies, waits for them, and re-layouts  4.8 us (6%)
    pallas_call x1, Pallas kernels, body(): pl.pallas_call(exchange_kernel, out_shape=[jax.ShapeDtypeStruct(outgoing....  40.3 us
    pallas_call x1, Pallas kernels, correlate_call(): pl.pallas_call(correlate_kernel, out_shape=jax.ShapeDtypeStruct((pair_row...  30.6 us
    unnamed x14, local copies, waits for them, and re-layouts  4.8 us
    pallas_call x1, Pallas kernels, body(): pl.pallas_call(prepare_kernel, out_shape=jax.ShapeDtypeStruct((device_cou...  2.36 us

profile of v2, /device:TPU:1, one launch (start us, length us, event | category | flops | bytes accessed | tf_op | source)
XLA Modules:
  0.0 79.2 jit_solution(16610979529106981716)
XLA Ops:
  0.0 0.0 copy-start.1
  0.0 1.0 %copy-done.1 = s32[4096,32]{0,1:T(8,128)S(1)} copy-done((s32[4096,32]{0,1:T(8,128)S(1)}, s32[4096,32]{0,1:T(8,128)}, u32[]{:S(2)}) %copy-start.1) | copy-done | bytes 524312
  1.0 0.0 copy-start.4
  1.0 0.7 copy-done.4
  1.8 1.1 %lookup.1 = s32[64,128]{1,0:T(8,128)S(1)} custom-call(s32[32,128]{1,0:T(8,128)S(1)} %bitcast.13, s32[32,4096]{1,0:T(8,128)S(1)} %bitcast.12), custom_call_target="tpu_custom_call" | custom-call | tf_op jit(solution)/shard_map/lookup/pallas_call | solution.py:370
  2.8 0.0 copy-start
  2.9 1.4 %copy-done = bf16[32,16,3,400]{3,1,2,0:T(8,128)(2,1)S(1)} copy-done((bf16[32,16,3,400]{3,1,2,0:T(8,128)(2,1)S(1)}, bf16[32,16,3,400]{3,1,2,0:T(8,128)(2,1)}, u32[]{:S(2)}) %copy-start) | copy-done | bytes 1228824
  4.3 0.0 copy-start.2
  4.3 0.9 %copy-done.2 = bf16[400,256]{1,0:T(8,128)(2,1)S(1)} copy-done((bf16[400,256]{1,0:T(8,128)(2,1)S(1)}, bf16[400,256]{1,0:T(8,128)(2,1)}, u32[]{:S(2)}) %copy-start.2) | copy-done | bytes 204824
  5.2 0.0 copy-start.5
  5.2 0.7 copy-done.5
  5.9 2.4 %prepare.1.out_ref = bf16[128,48,128]{2,1,0:T(8,128)(2,1)S(1)} custom-call(s32[4096]{0:T(1024)S(1)} %copy-done.4, bf16[1536,400]{1,0:T(8,128)(2,1)S(1)} %bitcast.9, s32[16,32]{1,0:T(8,128)S(1)} %bitcast.14, bf16[400,256]{1,0:T(8,128)(2,1)S(1)} %copy-done.2), custom_call_target="tpu_custom_call" | custom-call | tf_op jit(solution)/shard_map/prepare/pallas_call | solution.py:352
  8.3 0.0 copy-start.3
  8.3 0.0 copy-start.6
  8.3 40.3 %exchange.1 = (bf16[128,48,128]{2,1,0:T(8,128)(2,1)S(1)}, bf16[128,48,128]{2,1,0:T(8,128)(2,1)S(1)}) custom-call(bf16[128,48,128]{2,1,0:T(8,128)(2,1)S(1)} %prepare.1.out_ref), custom_call_target="tpu_custom_call" | custom-call | tf_op jit(solution)/shard_map/exchange/pallas_call | solution.py:379
  48.6 0.0 copy-done.3
  48.6 0.0 copy-done.6
  48.6 30.6 %correlate.1 = bf16[32768,128]{1,0:T(8,128)(2,1)} custom-call(s32[64,128]{1,0:T(8,128)S(1)} %lookup.1, s32[16]{0:T(128)S(1)} %copy-done.6, bf16[6144,128]{1,0:T(8,128)(2,1)S(1)} %bitcast.10, bf16[6144,128]{1,0:T(8,128)(2,1)S(1)} %bitcast.11, bf16[256,128]{1,0:T(8,128)(2,1)S(1)} %copy-done.3), custom_call_target="tpu_custom_call" | custom-call | tf_op jit(solution)/shard_map/correlate/pallas_call | solution.py:327
Async XLA Ops:
  0.0 1.0 %copy-start.1 = (s32[4096,32]{0,1:T(8,128)S(1)}, s32[4096,32]{0,1:T(8,128)}, u32[]{:S(2)}) copy-start(s32[4096,32]{0,1:T(8,128)} %param.11) | copy-start | bytes 1572868
  1.0 0.7 copy-start.4
  2.8 1.4 %copy-start = (bf16[32,16,3,400]{3,1,2,0:T(8,128)(2,1)S(1)}, bf16[32,16,3,400]{3,1,2,0:T(8,128)(2,1)}, u32[]{:S(2)}) copy-start(bf16[32,16,3,400]{3,1,2,0:T(8,128)(2,1)} %param.7) | copy-start | bytes 3686404
  4.3 0.9 %copy-start.2 = (bf16[400,256]{1,0:T(8,128)(2,1)S(1)}, bf16[400,256]{1,0:T(8,128)(2,1)}, u32[]{:S(2)}) copy-start(bf16[400,256]{1,0:T(8,128)(2,1)} %constant.4.clone.table_ref) | copy-start | bytes 614404
  5.2 0.7 copy-start.5
  8.3 40.3 %copy-start.3 = (bf16[256,128]{1,0:T(8,128)(2,1)S(1)}, bf16[256,128]{1,0:T(8,128)(2,1)}, u32[]{:S(2)}) copy-start(bf16[256,128]{1,0:T(8,128)(2,1)} %constant.5.clone.lag_ref) | copy-start | bytes 196612
  8.3 40.3 %copy-start.6 = (s32[16]{0:T(128)S(1)}, s32[16]{0:T(128)}, u32[]{:S(2)}) copy-start(s32[16]{0:T(128)} %band_ref.1) | copy-start | bytes 196

commit v3 on v2

v3 whole, which is shorter than its diff:
```python
import functools
import math

import jax
import jax.numpy as jnp
import numpy as np
from jax import lax
from jax.experimental import pallas as pl
from jax.experimental.pallas import tpu as pltpu
from jax.sharding import PartitionSpec as P

L = 400
COMP = 3
K = 128
K0 = 16
LAGS = 128
EPSILON = 1e-06

EVENTS = 4096
BLOCK = 32
NB = 32
CAP = 2
STATIONS = 16
GROUP = 4
ROWS = COMP * GROUP * 2
TILE = GROUP * 2
PER_DOT = 4
PER_STEP = 32


def forward_table():
    samples = np.arange(L, dtype=np.int32)
    bins = np.arange(K, dtype=np.int32) + K0
    turns = samples[:, None] * bins[None, :] % (2 * L)
    phase = turns.astype(np.float32) * np.float32(math.pi / L)
    taper = np.float32(0.5) - np.float32(0.5) * np.cos(
        (samples.astype(np.float32) + np.float32(0.5)) * np.float32(2.0 * math.pi / L)
    )
    table = np.concatenate(
        [taper[:, None] * np.cos(phase), -taper[:, None] * np.sin(phase)], axis=1
    )
    return table.astype(jnp.bfloat16)


def inverse_table():
    bins = np.arange(K, dtype=np.int32) + K0
    shifts = np.arange(LAGS, dtype=np.int32) - LAGS // 2
    turns = np.remainder(bins[:, None] * shifts[None, :], 2 * L)
    phase = turns.astype(np.float32) * np.float32(math.pi / L)
    return np.concatenate([np.cos(phase), -np.sin(phase)], axis=0).astype(jnp.bfloat16)


def position(shard):
    y, x, z, core = shard // 32, shard // 8 % 4, shard // 2 % 4, shard % 2
    return ((z * 4 + y) * 4 + x) * 2 + core


def index_kernel(owner_ref, partners_ref, out_ref):
    mine = lax.axis_index("clus")
    own = owner_ref[...]
    lane = lax.broadcasted_iota(jnp.int32, own.shape, 1)
    inside = lane % BLOCK
    rank = jnp.zeros(own.shape, jnp.int32)
    for d in range(1, BLOCK):
        same = (pltpu.roll(own, d, 1) == own) & (inside >= d)
        rank = rank + same.astype(jnp.int32)
    row = lax.broadcasted_iota(jnp.int32, own.shape, 0)
    rank_word = jnp.sum(rank << row, axis=0, keepdims=True)
    far_word = jnp.sum((own != mine).astype(jnp.int32) << row, axis=0, keepdims=True)
    total = jnp.zeros((2 * CAP * NB, 128), jnp.float32)
    shard_of_lane = lax.broadcasted_iota(jnp.int32, (128, 128), 0) // BLOCK
    shard = lax.broadcasted_iota(jnp.int32, (128, 128), 1)
    for t in range(own.shape[0]):
        p = partners_ref[:, t * 128 : (t + 1) * 128]
        high, low = p // 128, p % 128
        parts = []
        for r in range(CAP):
            take = (own[t : t + 1, :] == mine) & (rank[t : t + 1, :] == r)
            for half in (high, low):
                parts.append(jnp.where(take, half, 0).astype(jnp.float32))
        stacked = jnp.concatenate(parts, axis=0).astype(jnp.bfloat16)
        spread = (shard_of_lane + t * (128 // BLOCK) == shard).astype(jnp.float32)
        total = total + jnp.dot(
            stacked, spread.astype(jnp.bfloat16), preferred_element_type=jnp.float32
        )
    for r in range(CAP):
        high = total[2 * r * NB : (2 * r + 1) * NB].astype(jnp.int32)
        low = total[(2 * r + 1) * NB : (2 * r + 2) * NB].astype(jnp.int32)
        rank_bits = jnp.take_along_axis(jnp.broadcast_to(rank_word, low.shape), low, axis=1)
        far_bits = jnp.take_along_axis(jnp.broadcast_to(far_word, low.shape), low, axis=1)
        rank_bit = lax.shift_right_logical(rank_bits, high) & 1
        far_bit = lax.shift_right_logical(far_bits, high) & 1
        source = high * (128 // BLOCK) + low // BLOCK
        slot = far_bit * 256 + position(source) * CAP + rank_bit
        out_ref[r * NB : (r + 1) * NB, :] = slot * ROWS


MESH = pl.DeviceIdType.MESH
GROUPS = [
    (2, 2), (2, 1), (1, 2), (2, 3), (3, 2), (1, 1), (3, 3), (1, 3),
    (3, 1), (2, 0), (0, 2), (1, 0), (0, 1), (3, 0), (0, 3), (0, 0),
]
SHARE = 8
CHUNKS = 8


def slots_of_shard(owner_ref, source, slot_ref):
    per_row = 128 // BLOCK
    own = jnp.broadcast_to(owner_ref[pl.ds(source // per_row, 1), :], (128, 128))
    row = lax.broadcasted_iota(jnp.int32, (128, 128), 0)
    lane = lax.broadcasted_iota(jnp.int32, (128, 128), 1)
    column = jnp.sum(jnp.where(row == lane, own, 0), axis=1, keepdims=True)
    earlier = (column == own) & (row // BLOCK == lane // BLOCK) & (row < lane)
    rank = jnp.sum(earlier.astype(jnp.int32), axis=0, keepdims=True)
    slot = own[:1] * CAP + rank
    slot = jnp.where(lane[:1] // BLOCK == source % per_row, slot, -1)
    count = slot_ref.shape[0]
    hit = jnp.broadcast_to(slot, (count, 128)) == row[:count]
    event = jnp.sum(jnp.where(hit, lane[:count] % BLOCK + 1, 0), axis=1, keepdims=True) - 1
    slot_ref[...] = jnp.broadcast_to(event, (count, 128))


def exchange_kernel(
    owner_ref, windows_hbm, mask_ref, forward_ref, table_ref,
    windows, spectra, out_ref, own_ref, next_ref, slot_ref, slots,
    input_sem, slot_sem, send_sem, extra_sem, own_sem, next_sem,
    to_next_sem, to_own_sem, from_own_sem, from_next_sem,
):
    y = lax.axis_index("arch")
    me = lax.axis_index("clus")
    clus = lax.axis_size("clus")
    arch = lax.axis_size("arch")
    x, z, core = me // 8, me // 2 % 4, me % 2
    before, after = lax.rem(me + clus - 1, clus), lax.rem(me + 1, clus)
    after_z = after // 2 % 4
    after_core = x * 8 + lax.rem(z + 1, 4) * 2
    here = ((z * arch + y) * 4 + x) * 2 + core
    source = y * clus + me

    part = windows.shape[0] // CHUNKS
    loads = []
    for n in range(CHUNKS):
        some = pl.ds(n * part, part)
        loads.append(
            pltpu.make_async_copy(windows_hbm.at[some], windows.at[some], input_sem.at[n])
        )
        loads[-1].start()

    barrier = pltpu.get_barrier_semaphore()

    def greet(i, carry):
        other = lax.rem(source + i, arch * clus)
        pl.semaphore_signal(
            barrier, inc=1, device_id=(other // clus, lax.rem(other, clus)), device_id_type=MESH
        )
        return carry

    lax.fori_loop(1, arch * clus, greet, 0)

    slots_of_shard(owner_ref, source, slot_ref)
    fetch = pltpu.make_async_copy(slot_ref, slots, slot_sem)
    fetch.start()

    mask = mask_ref[...].astype(jnp.float32)
    forward = forward_ref[...]
    per = BLOCK // CHUNKS
    for n in range(CHUNKS):
        loads[n].wait()
        spec = jnp.dot(
            windows[n * part : (n + 1) * part, :], forward, preferred_element_type=jnp.float32
        )
        for e in range(per):
            event = n * per + e
            keep = jnp.broadcast_to(mask[:, event : event + 1], (STATIONS, K))
            for c in range(COMP):
                at = (e * COMP + c) * STATIONS
                to = (event * COMP + c) * (STATIONS // GROUP)
                real = spec[at : at + STATIONS, :K] * keep
                imag = spec[at : at + STATIONS, K:] * keep
                for a in range(STATIONS // GROUP):
                    some = slice(a * GROUP, (a + 1) * GROUP)
                    spectra[to + a, :GROUP, :] = real[some]
                    spectra[to + a, GROUP:, :] = imag[some]
    fetch.wait()

    def fill(o, carry):
        parts = [[], [], [], []]
        for r in range(CAP):
            e = slots[o * CAP + r, 0]
            valid = jnp.where(e >= 0, 1.0, 0.0).astype(jnp.float32)
            base = jnp.maximum(e, 0) * (COMP * STATIONS // GROUP)
            for c in range(COMP):
                for a in range(STATIONS // GROUP):
                    parts[a].append(spectra[base + (c * STATIONS // GROUP + a)] * valid)
        for a in range(STATIONS // GROUP):
            out_ref[a * clus + o] = jnp.concatenate(parts[a], axis=0).astype(jnp.bfloat16)
        return carry

    lax.fori_loop(0, clus, fill, 0)
    pl.semaphore_wait(barrier, arch * clus - 1)

    def issue(dz, dy):
        stays = dz in (0, 3)
        buffer, sems = (own_ref, own_sem) if stays else (next_ref, next_sem)
        sem = sems.at[((0 if dz == 0 else 1) if stays else dz - 1) * 4 + dy]
        to_y, to_z = lax.rem(y + dy, arch), lax.rem(z + dz, 4)

        def send(m, carry):
            owner = lax.rem(x + m // 2, 4) * 8 + to_z * 2 + m % 2
            target = owner if stays else lax.rem(owner + clus - 1, clus)
            block = out_ref.at[to_y * clus + owner]

            def remote(done):
                pltpu.make_async_remote_copy(
                    block,
                    buffer.at[here],
                    done,
                    sem,
                    device_id=(to_y, target),
                    device_id_type=MESH,
                ).start()

            if dy == 0 and dz in (0, 1):
                @pl.when(target == me)
                def _():
                    pltpu.make_async_copy(block, buffer.at[here], sem).start()

                single = (core == 0) & (owner == after_core) if dz == 1 else False

                @pl.when((target != me) & single)
                def _():
                    remote(extra_sem)

                @pl.when((target != me) & jnp.logical_not(single))
                def _():
                    remote(send_sem)
            else:
                remote(send_sem)
            return carry

        lax.fori_loop(0, SHARE, send, 0)

    for dz, dy in GROUPS:
        issue(dz, dy)

    def normalize(ref, at, first):
        def one(i, carry):
            block = ref[at + i].astype(jnp.float32)
            for e in range(CAP):
                parts = [
                    block[e * ROWS + c * TILE : e * ROWS + (c + 1) * TILE] for c in range(COMP)
                ]
                power = parts[0] * parts[0] + parts[1] * parts[1] + parts[2] * parts[2]
                power = power + pltpu.roll(power, GROUP, 0)
                energy = jnp.sum(power, axis=1, keepdims=True) * (1.0 / (COMP * 2 * K))
                scale = lax.rsqrt(energy + EPSILON)
                for c in range(COMP):
                    to = (first + at + i) * (CAP * ROWS) + e * ROWS + c * TILE
                    table_ref[pl.ds(pl.multiple_of(to, TILE), TILE), :] = parts[c] * scale
            return carry

        lax.fori_loop(0, SHARE, one, 0, unroll=SHARE)

    shards = arch * clus

    def place(z_of, k):
        return (lax.rem(z_of + 4, 4) * arch + lax.rem(y - k % 4 + arch, arch)) * SHARE

    def waited(ref, sem):
        pltpu.make_async_copy(ref, ref, sem).wait()

    def pass_on(i, carry):
        k = (1 - i // 4 % 2) * 4 + (2 + 3 * i) % 4
        is_own = (i < 8) == (core == 0)

        @pl.when(is_own)
        def _():
            at = place(z + k // 4, k)
            block = own_ref.at[pl.ds(at, SHARE)]
            waited(block, own_sem.at[k])
            pltpu.make_async_remote_copy(
                block,
                next_ref.at[pl.ds(at, SHARE)],
                to_next_sem.at[k],
                from_own_sem.at[k],
                device_id=(y, before),
                device_id_type=MESH,
            ).start()
            normalize(own_ref, at, 0)

        @pl.when(jnp.logical_not(is_own))
        def _():
            at = place(after_z - 1 - k // 4, k)
            block = next_ref.at[pl.ds(at, SHARE)]
            waited(block, next_sem.at[k])
            pltpu.make_async_remote_copy(
                block,
                own_ref.at[pl.ds(at, SHARE)],
                to_own_sem.at[k],
                from_next_sem.at[k],
                device_id=(y, after),
                device_id_type=MESH,
            ).start()
            normalize(next_ref, at, shards)

        return carry

    lax.fori_loop(0, 16, pass_on, 0)

    def take(i, carry):
        k = (1 - i // 4 % 2) * 4 + (2 + 3 * i) % 4
        is_own = (i < 8) == (core == 1)

        @pl.when(is_own)
        def _():
            at = place(z - 1 - k // 4, k)
            waited(own_ref.at[pl.ds(at, SHARE)], from_next_sem.at[k])
            normalize(own_ref, at, 0)

        @pl.when(jnp.logical_not(is_own))
        def _():
            at = place(after_z + k // 4, k)
            waited(next_ref.at[pl.ds(at, SHARE)], from_own_sem.at[k])
            normalize(next_ref, at, shards)

        return carry

    lax.fori_loop(0, 16, take, 0)

    def sent(k, carry):
        waited(own_ref.at[pl.ds(0, SHARE)], to_next_sem.at[k])
        waited(next_ref.at[pl.ds(0, SHARE)], to_own_sem.at[k])
        return carry

    lax.fori_loop(0, 8, sent, 0)
    waited(out_ref.at[pl.ds(0, shards - 2)], send_sem)

    @pl.when(core == 0)
    def _():
        waited(out_ref.at[0], extra_sem)


def correlate_kernel(lookup, band_ref, table, lag_ref, out_ref):
    step = pl.program_id(0)
    row = lax.broadcasted_iota(jnp.int32, (TILE, 128), 0)
    top = row < GROUP
    sign = jnp.where(top, 1.0, -1.0).astype(jnp.float32)
    band = jnp.zeros((TILE, 128), jnp.float32)
    first = lax.axis_index("arch") * GROUP
    for s in range(GROUP):
        member = band_ref[first + s].astype(jnp.float32) * (1.0 / (2.0 * COMP * K))
        band = jnp.where(row % GROUP == s, member, band)
    lag = lag_ref[...]
    rows = NB * GROUP
    for i in range(0, PER_STEP, PER_DOT):
        pairs = []
        for d in range(PER_DOT):
            shard = step * (PER_STEP // CAP) + (i + d) // CAP
            near = position(shard) * CAP + (i + d) % CAP
            direct, turned = [], []
            for c in range(COMP):
                at = pl.multiple_of(near * ROWS + c * TILE, TILE)
                piece = table[pl.ds(at, TILE), :] * band
                direct.append(piece)
                turned.append(pltpu.roll(piece, GROUP, 0) * sign)
            for j in range(NB):
                base = lookup[((i + d) % CAP) * NB + j, shard]
                v = [
                    table[pl.ds(pl.multiple_of(base + c * TILE, TILE), TILE), :]
                    for c in range(COMP)
                ]
                real = direct[0] * v[0] + direct[1] * v[1] + direct[2] * v[2]
                imag = turned[0] * v[0] + turned[1] * v[1] + turned[2] * v[2]
                pairs.append((real, imag))
        cross = []
        for p, q in zip(pairs[::2], pairs[1::2]):
            real = jnp.concatenate([p[0], q[0]], axis=0)
            imag = jnp.concatenate([p[1], q[1]], axis=0)
            cross.append(jnp.concatenate([real, imag], axis=1).astype(jnp.bfloat16))
        wide = jnp.dot(jnp.concatenate(cross, axis=0), lag, preferred_element_type=jnp.float32)
        merged = []
        for g in range(len(cross)):
            p = wide[2 * g * TILE : (2 * g + 1) * TILE]
            q = wide[(2 * g + 1) * TILE : (2 * g + 2) * TILE]
            merged.append(jnp.where(top, p, q) + pltpu.roll(jnp.where(top, q, p), GROUP, 0))
        lagged = jnp.concatenate(merged, axis=0).astype(jnp.bfloat16)
        out_ref[i * rows : (i + PER_DOT) * rows, :] = lagged


def correlate_call(lookup, band_member, table):
    vmem = pl.BlockSpec(memory_space=pltpu.VMEM)
    smem = pl.BlockSpec(memory_space=pltpu.SMEM)
    slots = table.shape[0] // (2 * ROWS)
    pair_rows = slots * NB * GROUP
    block_rows = PER_STEP * NB * GROUP
    result = pl.pallas_call(
        correlate_kernel,
        out_shape=jax.ShapeDtypeStruct((pair_rows, LAGS), jnp.bfloat16),
        grid=(slots // PER_STEP,),
        in_specs=[smem, smem, vmem, vmem],
        out_specs=pl.BlockSpec((block_rows, LAGS), lambda i: (i, 0)),
        compiler_params=pltpu.CompilerParams(vmem_limit_bytes=24 * 1024 * 1024),
        name="correlate",
    )(lookup, band_member, table, jnp.asarray(inverse_table()))
    return result.reshape(slots, NB, GROUP, LAGS)


def body(windows, pick_mask, band_member, event_owner, partners):
    arch_count = lax.axis_size("arch")
    clus_count = lax.axis_size("clus")
    shards = arch_count * clus_count
    vmem = pl.BlockSpec(memory_space=pltpu.VMEM)
    anywhere = pl.BlockSpec(memory_space=pl.ANY)
    limit = 24 * 1024 * 1024

    rows = BLOCK * COMP * STATIONS
    owners = event_owner.reshape(EVENTS // 128, 128)
    block = pltpu.VMEM((shards, CAP * ROWS, 128), jnp.bfloat16)
    dma = pltpu.SemaphoreType.DMA
    table = pl.pallas_call(
        exchange_kernel,
        out_shape=jax.ShapeDtypeStruct((2 * shards * CAP * ROWS, 128), jnp.float32),
        in_specs=[vmem, anywhere, vmem, vmem],
        out_specs=vmem,
        scratch_shapes=[
            pltpu.VMEM((rows, L), jnp.bfloat16),
            pltpu.VMEM((rows * 2 // TILE, TILE, K), jnp.float32),
            block,
            block,
            block,
            pltpu.VMEM((clus_count * CAP, 128), jnp.int32),
            pltpu.SMEM((clus_count * CAP, 128), jnp.int32),
            dma((CHUNKS,)),
            dma,
            dma,
            dma,
        ]
        + [dma((8,))] * 6,
        compiler_params=pltpu.CompilerParams(
            collective_id=0, has_side_effects=True, vmem_limit_bytes=limit
        ),
        name="exchange",
    )(
        owners,
        jnp.transpose(windows, (0, 2, 1, 3)).reshape(rows, L),
        pick_mask.T,
        jnp.asarray(forward_table()),
    )
    lookup = pl.pallas_call(
        index_kernel,
        out_shape=jax.ShapeDtypeStruct((CAP * NB, shards), jnp.int32),
        in_specs=[vmem, vmem],
        out_specs=vmem,
        compiler_params=pltpu.CompilerParams(vmem_limit_bytes=limit),
        name="lookup",
    )(owners, partners.T)
    return correlate_call(lookup, band_member, table)


def solution(mesh):
    return jax.shard_map(
        body,
        mesh=mesh,
        in_specs=(P(("arch", "clus"), None, None, None), P(("arch", "clus"), None), P(), P(), P()),
        out_specs=P("clus", None, "arch", None),
        check_vma=False,
    )
```

time: 79.5 us -> 67.3 us (0.85)
  Pallas kernels: 74.3 us -> 62.2 us
    pallas_call x1, Pallas kernels: 30.6 us -> 18.7 us  [correlate_call(): pl.pallas_call(correlate_kernel, out_shape=jax.ShapeDtypeStruct((pair_row...]
    pallas_call x3 -> x2, Pallas kernels: 43.7 us -> 43.5 us  [the longest x1 42.4 us: body(): pl.pallas_call(exchange_kernel, out_shape=jax.ShapeDtypeStruct((2 * shard...]
where the time goes in v3:
time: 67.3 us; the launch traced here: 67 us
  Pallas kernels  62.2 us (92%)
  local copies, waits for them, and re-layouts  4.81 us (7%)
    pallas_call x1, Pallas kernels, body(): pl.pallas_call(exchange_kernel, out_shape=jax.ShapeDtypeStruct((2 * shard...  42.4 us
    pallas_call x1, Pallas kernels, correlate_call(): pl.pallas_call(correlate_kernel, out_shape=jax.ShapeDtypeStruct((pair_row...  18.7 us
    unnamed x14, local copies, waits for them, and re-layouts  4.81 us

profile of v3, /device:TPU:1, one launch (start us, length us, event | category | flops | bytes accessed | tf_op | source)
XLA Modules:
  0.0 67.0 jit_solution(16746203786467664109)
XLA Ops:
  0.0 0.0 copy-start.6
  0.0 0.0 copy-start.1
  0.0 1.1 %copy-done.1 = s32[4096,32]{0,1:T(8,128)S(1)} copy-done((s32[4096,32]{0,1:T(8,128)S(1)}, s32[4096,32]{0,1:T(8,128)}, u32[]{:S(2)}) %copy-start.1) | copy-done | bytes 524312
  1.1 0.0 copy-start.4
  1.1 0.7 %copy-done.4 = s32[4096]{0:T(1024)S(1)} copy-done((s32[4096]{0:T(1024)S(1)}, s32[4096]{0:T(1024)}, u32[]{:S(2)}) %copy-start.4) | copy-done | bytes 16408
  1.8 0.0 copy-start.3
  1.8 1.1 %lookup.1 = s32[64,128]{1,0:T(8,128)S(1)} custom-call(s32[32,128]{1,0:T(8,128)S(1)} %bitcast.9, s32[32,4096]{1,0:T(8,128)S(1)} %bitcast.8), custom_call_target="tpu_custom_call" | custom-call | tf_op jit(solution)/shard_map/lookup/pallas_call | solution.py:449
  2.9 0.0 copy-start
  2.9 1.4 %copy-done = bf16[32,16,3,400]{3,1,2,0:T(8,128)(2,1)S(1)} copy-done((bf16[32,16,3,400]{3,1,2,0:T(8,128)(2,1)S(1)}, bf16[32,16,3,400]{3,1,2,0:T(8,128)(2,1)}, u32[]{:S(2)}) %copy-start) | copy-done | bytes 1228824
  4.3 0.0 copy-start.2
  4.3 0.9 %copy-done.2 = bf16[400,256]{1,0:T(8,128)(2,1)S(1)} copy-done((bf16[400,256]{1,0:T(8,128)(2,1)S(1)}, bf16[400,256]{1,0:T(8,128)(2,1)}, u32[]{:S(2)}) %copy-start.2) | copy-done | bytes 204824
  5.2 0.0 copy-start.5
  5.2 0.7 %copy-done.5 = s32[32,16]{0,1:T(8,128)S(1)} copy-done((s32[32,16]{0,1:T(8,128)S(1)}, s32[32,16]{0,1:T(8,128)}, u32[]{:S(2)}) %copy-start.5) | copy-done | bytes 2072
  5.9 42.4 %exchange.1.table = f32[12288,128]{1,0:T(8,128)S(1)} custom-call(s32[32,128]{1,0:T(8,128)S(1)} %bitcast.10, bf16[1536,400]{1,0:T(8,128)(2,1)S(1)} %bitcast.7, s32[16,32]{1,0:T(8,128)S(1)} %bitcast.11, bf16[400,256]{1,0:T(8,128)(2,1)S(1)} %copy-done.2), custom_call_target="tpu_custom_call" | custom-call | tf_op jit(solution)/shard_map/exchange/pallas_call | solution.py:420
  48.3 0.0 copy-done.6
  48.3 0.0 copy-done.3
  48.3 18.7 %correlate.1 = bf16[32768,128]{1,0:T(8,128)(2,1)} custom-call(s32[64,128]{1,0:T(8,128)S(1)} %lookup.1, s32[16]{0:T(128)S(1)} %copy-done.6, f32[12288,128]{1,0:T(8,128)S(1)} %exchange.1.table, bf16[256,128]{1,0:T(8,128)(2,1)S(1)} %copy-done.3), custom_call_target="tpu_custom_call" | custom-call | tf_op jit(solution)/shard_map/correlate/pallas_call | solution.py:396
Async XLA Ops:
  0.0 48.3 %copy-start.6 = (s32[16]{0:T(128)S(1)}, s32[16]{0:T(128)}, u32[]{:S(2)}) copy-start(s32[16]{0:T(128)} %band_ref.1) | copy-start | bytes 196
  0.0 1.1 %copy-start.1 = (s32[4096,32]{0,1:T(8,128)S(1)}, s32[4096,32]{0,1:T(8,128)}, u32[]{:S(2)}) copy-start(s32[4096,32]{0,1:T(8,128)} %param.11) | copy-start | bytes 1572868
  1.1 0.7 %copy-start.4 = (s32[4096]{0:T(1024)S(1)}, s32[4096]{0:T(1024)}, u32[]{:S(2)}) copy-start(s32[4096]{0:T(1024)} %param.10) | copy-start | bytes 49156
  1.8 46.5 %copy-start.3 = (bf16[256,128]{1,0:T(8,128)(2,1)S(1)}, bf16[256,128]{1,0:T(8,128)(2,1)}, u32[]{:S(2)}) copy-start(bf16[256,128]{1,0:T(8,128)(2,1)} %constant.5.clone.lag_ref) | copy-start | bytes 196612
  2.9 1.4 %copy-start = (bf16[32,16,3,400]{3,1,2,0:T(8,128)(2,1)S(1)}, bf16[32,16,3,400]{3,1,2,0:T(8,128)(2,1)}, u32[]{:S(2)}) copy-start(bf16[32,16,3,400]{3,1,2,0:T(8,128)(2,1)} %param.7) | copy-start | bytes 3686404
  4.3 0.9 %copy-start.2 = (bf16[400,256]{1,0:T(8,128)(2,1)S(1)}, bf16[400,256]{1,0:T(8,128)(2,1)}, u32[]{:S(2)}) copy-start(bf16[400,256]{1,0:T(8,128)(2,1)} %constant.4.clone.forward_ref) | copy-start | bytes 614404
  5.2 0.7 %copy-start.5 = (s32[32,16]{0,1:T(8,128)S(1)}, s32[32,16]{0,1:T(8,128)}, u32[]{:S(2)}) copy-start(s32[32,16]{0,1:T(8,128)} %param.8) | copy-start | bytes 6148

commit v4 on v3

--- a/solution.py
+++ b/solution.py
@@ -121,9 +121,9 @@
 
 
 def exchange_kernel(
-    owner_ref, windows_hbm, mask_ref, forward_ref, table_ref,
-    windows, spectra, out_ref, own_ref, next_ref, slot_ref, slots,
-    input_sem, slot_sem, send_sem, extra_sem, own_sem, next_sem,
+    owner_ref, windows, mask_ref, forward_ref, table_ref,
+    spectra, out_ref, own_ref, next_ref, slot_ref, slots,
+    slot_sem, send_sem, extra_sem, own_sem, next_sem,
     to_next_sem, to_own_sem, from_own_sem, from_next_sem,
 ):
     y = lax.axis_index("arch")
@@ -138,24 +138,17 @@
     source = y * clus + me
 
     part = windows.shape[0] // CHUNKS
-    loads = []
-    for n in range(CHUNKS):
-        some = pl.ds(n * part, part)
-        loads.append(
-            pltpu.make_async_copy(windows_hbm.at[some], windows.at[some], input_sem.at[n])
-        )
-        loads[-1].start()
-
     barrier = pltpu.get_barrier_semaphore()
-
-    def greet(i, carry):
-        other = lax.rem(source + i, arch * clus)
-        pl.semaphore_signal(
-            barrier, inc=1, device_id=(other // clus, lax.rem(other, clus)), device_id_type=MESH
-        )
-        return carry
-
-    lax.fori_loop(1, arch * clus, greet, 0)
+    for dy in range(4):
+        to_y = lax.rem(y + dy, arch)
+
+        def greet(i, carry, to_y=to_y):
+            to = me + i
+            to = jnp.where(to >= clus, to - clus, to)
+            pl.semaphore_signal(barrier, inc=1, device_id=(to_y, to), device_id_type=MESH)
+            return carry
+
+        lax.fori_loop(0 if dy else 1, clus, greet, 0, unroll=8 if dy else False)
 
     slots_of_shard(owner_ref, source, slot_ref)
     fetch = pltpu.make_async_copy(slot_ref, slots, slot_sem)
@@ -165,7 +158,6 @@
     forward = forward_ref[...]
     per = BLOCK // CHUNKS
     for n in range(CHUNKS):
-        loads[n].wait()
         spec = jnp.dot(
             windows[n * part : (n + 1) * part, :], forward, preferred_element_type=jnp.float32
         )
@@ -199,14 +191,14 @@
     lax.fori_loop(0, clus, fill, 0)
     pl.semaphore_wait(barrier, arch * clus - 1)
 
-    def issue(dz, dy):
+    def issue(owner_core, dz, dy):
         stays = dz in (0, 3)
         buffer, sems = (own_ref, own_sem) if stays else (next_ref, next_sem)
         sem = sems.at[((0 if dz == 0 else 1) if stays else dz - 1) * 4 + dy]
         to_y, to_z = lax.rem(y + dy, arch), lax.rem(z + dz, 4)
 
         def send(m, carry):
-            owner = lax.rem(x + m // 2, 4) * 8 + to_z * 2 + m % 2
+            owner = lax.rem(x + m, 4) * 8 + to_z * 2 + owner_core
             target = owner if stays else lax.rem(owner + clus - 1, clus)
             block = out_ref.at[to_y * clus + owner]
 
@@ -220,7 +212,7 @@
                     device_id_type=MESH,
                 ).start()
 
-            if dy == 0 and dz in (0, 1):
+            if dy == 0 and (dz == 0 or (dz == 1 and owner_core == 0)):
                 @pl.when(target == me)
                 def _():
                     pltpu.make_async_copy(block, buffer.at[here], sem).start()
@@ -238,10 +230,11 @@
                 remote(send_sem)
             return carry
 
-        lax.fori_loop(0, SHARE, send, 0)
-
-    for dz, dy in GROUPS:
-        issue(dz, dy)
+        lax.fori_loop(0, 4, send, 0)
+
+    for owner_core in range(2):
+        for dz, dy in GROUPS:
+            issue(owner_core, dz, dy)
 
     def normalize(ref, at, first):
         def one(i, carry):
@@ -269,12 +262,11 @@
     def waited(ref, sem):
         pltpu.make_async_copy(ref, ref, sem).wait()
 
-    def pass_on(i, carry):
-        k = (1 - i // 4 % 2) * 4 + (2 + 3 * i) % 4
-        is_own = (i < 8) == (core == 0)
-
-        @pl.when(is_own)
-        def _():
+    own_order = [(0 if dz == 0 else 4) + dy for dz, dy in GROUPS if dz in (0, 3)]
+    next_order = [(dz - 1) * 4 + dy for dz, dy in GROUPS if dz in (1, 2)]
+
+    def pass_own():
+        for k in own_order:
             at = place(z + k // 4, k)
             block = own_ref.at[pl.ds(at, SHARE)]
             waited(block, own_sem.at[k])
@@ -286,10 +278,9 @@
                 device_id=(y, before),
                 device_id_type=MESH,
             ).start()
-            normalize(own_ref, at, 0)
-
-        @pl.when(jnp.logical_not(is_own))
-        def _():
+
+    def pass_next():
+        for k in next_order:
             at = place(after_z - 1 - k // 4, k)
             block = next_ref.at[pl.ds(at, SHARE)]
             waited(block, next_sem.at[k])
@@ -301,11 +292,23 @@
                 device_id=(y, after),
                 device_id_type=MESH,
             ).start()
-            normalize(next_ref, at, shards)
-
+
+    @pl.when(core == 0)
+    def _():
+        pass_own()
+        pass_next()
+
+    @pl.when(core == 1)
+    def _():
+        pass_next()
+        pass_own()
+
+    def direct(k, carry):
+        normalize(own_ref, place(z + k // 4, k), 0)
+        normalize(next_ref, place(after_z - 1 - k // 4, k), shards)
         return carry
 
-    lax.fori_loop(0, 16, pass_on, 0)
+    lax.fori_loop(0, 8, direct, 0)
 
     def take(i, carry):
         k = (1 - i // 4 % 2) * 4 + (2 + 3 * i) % 4
@@ -410,7 +413,6 @@
     clus_count = lax.axis_size("clus")
     shards = arch_count * clus_count
     vmem = pl.BlockSpec(memory_space=pltpu.VMEM)
-    anywhere = pl.BlockSpec(memory_space=pl.ANY)
     limit = 24 * 1024 * 1024
 
     rows = BLOCK * COMP * STATIONS
@@ -420,17 +422,15 @@
     table = pl.pallas_call(
         exchange_kernel,
         out_shape=jax.ShapeDtypeStruct((2 * shards * CAP * ROWS, 128), jnp.float32),
-        in_specs=[vmem, anywhere, vmem, vmem],
+        in_specs=[vmem] * 4,
         out_specs=vmem,
         scratch_shapes=[
-            pltpu.VMEM((rows, L), jnp.bfloat16),
             pltpu.VMEM((rows * 2 // TILE, TILE, K), jnp.float32),
             block,
             block,
             block,
             pltpu.VMEM((clus_count * CAP, 128), jnp.int32),
             pltpu.SMEM((clus_count * CAP, 128), jnp.int32),
-            dma((CHUNKS,)),
             dma,
             dma,
             dma,

time: 67.3 us -> 63.9 us (0.949)
  Pallas kernels: 62.2 us -> 58.8 us
    pallas_call x1, Pallas kernels: 42.4 us -> 38.8 us  [body(): pl.pallas_call(exchange_kernel, out_shape=jax.ShapeDtypeStruct((2 * shard...]
where the time goes in v4:
time: 63.9 us; the launch traced here: 63.6 us
  Pallas kernels  58.8 us (92%)
  local copies, waits for them, and re-layouts  4.81 us (8%)
    pallas_call x1, Pallas kernels, body(): pl.pallas_call(exchange_kernel, out_shape=jax.ShapeDtypeStruct((2 * shard...  38.8 us
    pallas_call x1, Pallas kernels, correlate_call(): pl.pallas_call(correlate_kernel, out_shape=jax.ShapeDtypeStruct((pair_row...  18.9 us
    unnamed x14, local copies, waits for them, and re-layouts  4.81 us

profile of v4, /device:TPU:1, one launch (start us, length us, event | category | flops | bytes accessed | tf_op | source)
XLA Modules:
  0.0 63.6 jit_solution(15769130943719227984)
XLA Ops:
  0.0 0.0 copy-start.6
  0.0 0.0 copy-start.1
  0.0 1.1 %copy-done.1 = s32[4096,32]{0,1:T(8,128)S(1)} copy-done((s32[4096,32]{0,1:T(8,128)S(1)}, s32[4096,32]{0,1:T(8,128)}, u32[]{:S(2)}) %copy-start.1) | copy-done | bytes 524312
  1.1 0.0 copy-start.4
  1.1 0.7 %copy-done.4 = s32[4096]{0:T(1024)S(1)} copy-done((s32[4096]{0:T(1024)S(1)}, s32[4096]{0:T(1024)}, u32[]{:S(2)}) %copy-start.4) | copy-done | bytes 16408
  1.8 0.0 copy-start.3
  1.8 1.1 %lookup.1 = s32[64,128]{1,0:T(8,128)S(1)} custom-call(s32[32,128]{1,0:T(8,128)S(1)} %bitcast.9, s32[32,4096]{1,0:T(8,128)S(1)} %bitcast.8), custom_call_target="tpu_custom_call" | custom-call | tf_op jit(solution)/shard_map/lookup/pallas_call | solution.py:449
  2.9 0.0 copy-start
  2.9 1.4 %copy-done = bf16[32,16,3,400]{3,1,2,0:T(8,128)(2,1)S(1)} copy-done((bf16[32,16,3,400]{3,1,2,0:T(8,128)(2,1)S(1)}, bf16[32,16,3,400]{3,1,2,0:T(8,128)(2,1)}, u32[]{:S(2)}) %copy-start) | copy-done | bytes 1228824
  4.3 0.0 copy-start.2
  4.3 0.9 %copy-done.2 = bf16[400,256]{1,0:T(8,128)(2,1)S(1)} copy-done((bf16[400,256]{1,0:T(8,128)(2,1)S(1)}, bf16[400,256]{1,0:T(8,128)(2,1)}, u32[]{:S(2)}) %copy-start.2) | copy-done | bytes 204824
  5.2 0.0 copy-start.5
  5.2 0.7 %copy-done.5 = s32[32,16]{0,1:T(8,128)S(1)} copy-done((s32[32,16]{0,1:T(8,128)S(1)}, s32[32,16]{0,1:T(8,128)}, u32[]{:S(2)}) %copy-start.5) | copy-done | bytes 2072
  5.9 38.8 %exchange.1.table = f32[12288,128]{1,0:T(8,128)S(1)} custom-call(s32[32,128]{1,0:T(8,128)S(1)} %bitcast.10, bf16[1536,400]{1,0:T(8,128)(2,1)S(1)} %bitcast.7, s32[16,32]{1,0:T(8,128)S(1)} %bitcast.11, bf16[400,256]{1,0:T(8,128)(2,1)S(1)} %copy-done.2), custom_call_target="tpu_custom_call" | custom-call | tf_op jit(solution)/shard_map/exchange/pallas_call | solution.py:422
  44.7 0.0 copy-done.6
  44.7 0.0 copy-done.3
  44.7 18.9 %correlate.1 = bf16[32768,128]{1,0:T(8,128)(2,1)} custom-call(s32[64,128]{1,0:T(8,128)S(1)} %lookup.1, s32[16]{0:T(128)S(1)} %copy-done.6, f32[12288,128]{1,0:T(8,128)S(1)} %exchange.1.table, bf16[256,128]{1,0:T(8,128)(2,1)S(1)} %copy-done.3), custom_call_target="tpu_custom_call" | custom-call | tf_op jit(solution)/shard_map/correlate/pallas_call | solution.py:399
Async XLA Ops:
  0.0 44.7 %copy-start.6 = (s32[16]{0:T(128)S(1)}, s32[16]{0:T(128)}, u32[]{:S(2)}) copy-start(s32[16]{0:T(128)} %band_ref.1) | copy-start | bytes 196
  0.0 1.1 %copy-start.1 = (s32[4096,32]{0,1:T(8,128)S(1)}, s32[4096,32]{0,1:T(8,128)}, u32[]{:S(2)}) copy-start(s32[4096,32]{0,1:T(8,128)} %param.11) | copy-start | bytes 1572868
  1.1 0.7 %copy-start.4 = (s32[4096]{0:T(1024)S(1)}, s32[4096]{0:T(1024)}, u32[]{:S(2)}) copy-start(s32[4096]{0:T(1024)} %param.10) | copy-start | bytes 49156
  1.8 42.9 %copy-start.3 = (bf16[256,128]{1,0:T(8,128)(2,1)S(1)}, bf16[256,128]{1,0:T(8,128)(2,1)}, u32[]{:S(2)}) copy-start(bf16[256,128]{1,0:T(8,128)(2,1)} %constant.5.clone.lag_ref) | copy-start | bytes 196612
  2.9 1.4 %copy-start = (bf16[32,16,3,400]{3,1,2,0:T(8,128)(2,1)S(1)}, bf16[32,16,3,400]{3,1,2,0:T(8,128)(2,1)}, u32[]{:S(2)}) copy-start(bf16[32,16,3,400]{3,1,2,0:T(8,128)(2,1)} %param.7) | copy-start | bytes 3686404
  4.3 0.9 %copy-start.2 = (bf16[400,256]{1,0:T(8,128)(2,1)S(1)}, bf16[400,256]{1,0:T(8,128)(2,1)}, u32[]{:S(2)}) copy-start(bf16[400,256]{1,0:T(8,128)(2,1)} %constant.4.clone.forward_ref) | copy-start | bytes 614404
  5.2 0.7 %copy-start.5 = (s32[32,16]{0,1:T(8,128)S(1)}, s32[32,16]{0,1:T(8,128)}, u32[]{:S(2)}) copy-start(s32[32,16]{0,1:T(8,128)} %param.8) | copy-start | bytes 6148

commit v5 on v4

--- a/solution.py
+++ b/solution.py
@@ -24,8 +24,8 @@
 GROUP = 4
 ROWS = COMP * GROUP * 2
 TILE = GROUP * 2
-PER_DOT = 4
-PER_STEP = 32
+PER_DOT = 8
+PER_STEP = 64
 
 
 def forward_table():
@@ -55,8 +55,7 @@
     return ((z * 4 + y) * 4 + x) * 2 + core
 
 
-def index_kernel(owner_ref, partners_ref, out_ref):
-    mine = lax.axis_index("clus")
+def find_partners(mine, owner_ref, partners_ref, out_ref):
     own = owner_ref[...]
     lane = lax.broadcasted_iota(jnp.int32, own.shape, 1)
     inside = lane % BLOCK
@@ -121,8 +120,8 @@
 
 
 def exchange_kernel(
-    owner_ref, windows, mask_ref, forward_ref, table_ref,
-    spectra, out_ref, own_ref, next_ref, slot_ref, slots,
+    owner_ref, windows, mask_ref, forward_ref, partners_ref, table_ref, lookup_ref,
+    lag_ref, spectra, out_ref, own_ref, next_ref, slot_ref, slots,
     slot_sem, send_sem, extra_sem, own_sem, next_sem,
     to_next_sem, to_own_sem, from_own_sem, from_next_sem,
 ):
@@ -155,7 +154,9 @@
     fetch.start()
 
     mask = mask_ref[...].astype(jnp.float32)
-    forward = forward_ref[...]
+    forward = forward_ref[:L, :]
+    lag_ref[:K, :] = forward_ref[L:, :LAGS]
+    lag_ref[K:, :] = forward_ref[L:, LAGS:]
     per = BLOCK // CHUNKS
     for n in range(CHUNKS):
         spec = jnp.dot(
@@ -302,6 +303,8 @@
     def _():
         pass_next()
         pass_own()
+
+    find_partners(me, owner_ref, partners_ref, lookup_ref)
 
     def direct(k, carry):
         normalize(own_ref, place(z + k // 4, k), 0)
@@ -390,7 +393,7 @@
         out_ref[i * rows : (i + PER_DOT) * rows, :] = lagged
 
 
-def correlate_call(lookup, band_member, table):
+def correlate_call(lookup, band_member, table, lag):
     vmem = pl.BlockSpec(memory_space=pltpu.VMEM)
     smem = pl.BlockSpec(memory_space=pltpu.SMEM)
     slots = table.shape[0] // (2 * ROWS)
@@ -404,7 +407,7 @@
         out_specs=pl.BlockSpec((block_rows, LAGS), lambda i: (i, 0)),
         compiler_params=pltpu.CompilerParams(vmem_limit_bytes=24 * 1024 * 1024),
         name="correlate",
-    )(lookup, band_member, table, jnp.asarray(inverse_table()))
+    )(lookup, band_member, table, lag)
     return result.reshape(slots, NB, GROUP, LAGS)
 
 
@@ -419,11 +422,19 @@
     owners = event_owner.reshape(EVENTS // 128, 128)
     block = pltpu.VMEM((shards, CAP * ROWS, 128), jnp.bfloat16)
     dma = pltpu.SemaphoreType.DMA
-    table = pl.pallas_call(
+    lag_rows = inverse_table()
+    tables = np.concatenate(
+        [forward_table(), np.concatenate([lag_rows[:K], lag_rows[K:]], axis=1)], axis=0
+    )
+    table, lookup, lag = pl.pallas_call(
         exchange_kernel,
-        out_shape=jax.ShapeDtypeStruct((2 * shards * CAP * ROWS, 128), jnp.float32),
-        in_specs=[vmem] * 4,
-        out_specs=vmem,
+        out_shape=[
+            jax.ShapeDtypeStruct((2 * shards * CAP * ROWS, 128), jnp.float32),
+            jax.ShapeDtypeStruct((CAP * NB, shards), jnp.int32),
+            jax.ShapeDtypeStruct((2 * K, LAGS), jnp.bfloat16),
+        ],
+        in_specs=[vmem] * 5,
+        out_specs=[vmem] * 3,
         scratch_shapes=[
             pltpu.VMEM((rows * 2 // TILE, TILE, K), jnp.float32),
             block,
@@ -444,17 +455,10 @@
         owners,
         jnp.transpose(windows, (0, 2, 1, 3)).reshape(rows, L),
         pick_mask.T,
-        jnp.asarray(forward_table()),
+        jnp.asarray(tables),
+        partners.T,
     )
-    lookup = pl.pallas_call(
-        index_kernel,
-        out_shape=jax.ShapeDtypeStruct((CAP * NB, shards), jnp.int32),
-        in_specs=[vmem, vmem],
-        out_specs=vmem,
-        compiler_params=pltpu.CompilerParams(vmem_limit_bytes=limit),
-        name="lookup",
-    )(owners, partners.T)
-    return correlate_call(lookup, band_member, table)
+    return correlate_call(lookup, band_member, table, lag)
 
 
 def solution(mesh):

time: 63.9 us -> 62.9 us (0.984)
  Pallas kernels: 58.8 us -> 57 us
  local copies, waits for them, and re-layouts: 4.81 us -> 5.46 us
    pallas_call x2 -> x1, Pallas kernels: 39.8 us -> 38.8 us  [body(): pl.pallas_call(exchange_kernel, out_shape=[jax.ShapeDtypeStruct((2 * shar...]
    unnamed x14 -> x12, local copies, waits for them, and re-layouts: 4.81 us -> 5.46 us
    pallas_call x1, Pallas kernels: 18.9 us -> 18.3 us  [correlate_call(): pl.pallas_call(correlate_kernel, out_shape=jax.ShapeDtypeStruct((pair_row...]
where the time goes in v5:
time: 62.9 us; the launch traced here: 62.5 us
  Pallas kernels  57 us (91%)
  local copies, waits for them, and re-layouts  5.46 us (9%)
    pallas_call x1, Pallas kernels, body(): pl.pallas_call(exchange_kernel, out_shape=[jax.ShapeDtypeStruct((2 * shar...  38.8 us
    pallas_call x1, Pallas kernels, correlate_call(): pl.pallas_call(correlate_kernel, out_shape=jax.ShapeDtypeStruct((pair_row...  18.3 us
    unnamed x12, local copies, waits for them, and re-layouts  5.46 us

profile of v5, /device:TPU:1, one launch (start us, length us, event | category | flops | bytes accessed | tf_op | source)
XLA Modules:
  0.0 62.5 jit_solution(5652041790901007170)
XLA Ops:
  0.0 0.0 copy-start
  0.0 1.4 %copy-done = bf16[32,16,3,400]{3,1,2,0:T(8,128)(2,1)S(1)} copy-done((bf16[32,16,3,400]{3,1,2,0:T(8,128)(2,1)S(1)}, bf16[32,16,3,400]{3,1,2,0:T(8,128)(2,1)}, u32[]{:S(2)}) %copy-start) | copy-done | bytes 1228824
  1.4 0.0 copy-start.1
  1.4 1.0 %copy-done.1 = s32[4096,32]{0,1:T(8,128)S(1)} copy-done((s32[4096,32]{0,1:T(8,128)S(1)}, s32[4096,32]{0,1:T(8,128)}, u32[]{:S(2)}) %copy-start.1) | copy-done | bytes 524312
  2.5 0.0 copy-start.2
  2.5 1.0 %copy-done.2 = bf16[528,256]{1,0:T(8,128)(2,1)S(1)} copy-done((bf16[528,256]{1,0:T(8,128)(2,1)S(1)}, bf16[528,256]{1,0:T(8,128)(2,1)}, u32[]{:S(2)}) %copy-start.2) | copy-done | bytes 270360
  3.4 0.0 copy-start.3
  3.4 0.7 %copy-done.3 = s32[4096]{0:T(1024)S(1)} copy-done((s32[4096]{0:T(1024)S(1)}, s32[4096]{0:T(1024)}, u32[]{:S(2)}) %copy-start.3) | copy-done | bytes 16408
  4.1 0.0 copy-start.4
  4.1 0.7 %copy-done.4 = s32[32,16]{0,1:T(8,128)S(1)} copy-done((s32[32,16]{0,1:T(8,128)S(1)}, s32[32,16]{0,1:T(8,128)}, u32[]{:S(2)}) %copy-start.4) | copy-done | bytes 2072
  4.8 38.8 %exchange.1 = (f32[12288,128]{1,0:T(8,128)S(1)}, s32[64,128]{1,0:T(8,128)S(1)}, bf16[256,128]{1,0:T(8,128)(2,1)S(1)}) custom-call(s32[32,128]{1,0:T(8,128)S(1)} %bitcast.9, bf16[1536,400]{1,0:T(8,128)(2,1)S(1)} %bitcast.7, s32[16,32]{1,0:T(8,128)S(1)} %bitcast.10, bf16[528,256]{1,0:T(8,128)(2,1)S(1)} %copy-done.2, s32[32,4096]{1,0:T(8,128)S(1)} %bitcast.8), custom_call_target="tpu_custom_call" | custom-call | tf_op jit(solution)/shard_map/exchange/pallas_call | solution.py:429
  43.6 0.0 copy-start.5
  43.6 0.6 %copy-done.5 = s32[16]{0:T(128)S(1)} copy-done((s32[16]{0:T(128)S(1)}, s32[16]{0:T(128)}, u32[]{:S(2)}) %copy-start.5) | copy-done | bytes 88
  44.2 18.3 %correlate.1 = bf16[32768,128]{1,0:T(8,128)(2,1)} custom-call(s32[64,128]{1,0:T(8,128)S(1)} %get-tuple-element.8.lookup, s32[16]{0:T(128)S(1)} %copy-done.5, f32[12288,128]{1,0:T(8,128)S(1)} %get-tuple-element.9.table, bf16[256,128]{1,0:T(8,128)(2,1)S(1)} %get-tuple-element.10.lag_ref), custom_call_target="tpu_custom_call" | custom-call | tf_op jit(solution)/shard_map/correlate/pallas_call | solution.py:402
Async XLA Ops:
  0.0 1.4 %copy-start = (bf16[32,16,3,400]{3,1,2,0:T(8,128)(2,1)S(1)}, bf16[32,16,3,400]{3,1,2,0:T(8,128)(2,1)}, u32[]{:S(2)}) copy-start(bf16[32,16,3,400]{3,1,2,0:T(8,128)(2,1)} %param.6) | copy-start | bytes 3686404
  1.4 1.0 %copy-start.1 = (s32[4096,32]{0,1:T(8,128)S(1)}, s32[4096,32]{0,1:T(8,128)}, u32[]{:S(2)}) copy-start(s32[4096,32]{0,1:T(8,128)} %param.10) | copy-start | bytes 1572868
  2.5 1.0 %copy-start.2 = (bf16[528,256]{1,0:T(8,128)(2,1)S(1)}, bf16[528,256]{1,0:T(8,128)(2,1)}, u32[]{:S(2)}) copy-start(bf16[528,256]{1,0:T(8,128)(2,1)} %constant.2.clone.forward_ref) | copy-start | bytes 811012
  3.4 0.7 %copy-start.3 = (s32[4096]{0:T(1024)S(1)}, s32[4096]{0:T(1024)}, u32[]{:S(2)}) copy-start(s32[4096]{0:T(1024)} %param.9) | copy-start | bytes 49156
  4.1 0.7 %copy-start.4 = (s32[32,16]{0,1:T(8,128)S(1)}, s32[32,16]{0,1:T(8,128)}, u32[]{:S(2)}) copy-start(s32[32,16]{0,1:T(8,128)} %param.7) | copy-start | bytes 6148
  43.6 0.7 %copy-start.5 = (s32[16]{0:T(128)S(1)}, s32[16]{0:T(128)}, u32[]{:S(2)}) copy-start(s32[16]{0:T(128)} %band_ref.1) | copy-start | bytes 196
